TPU v7x, 256 devices: a whole 4x4x8 slice. The times are simulated.
256 devices in a mesh: tm: 32 (over x, z), space: 8 (over y, core).
Axes of the slice: x: 4, y: 4, z: 8, core: 2. Of those that a mesh axis runs over, the one named last changes fastest.
Arguments:
- state: float32 [64, 4, 64, 1024], P('tm', None, 'space'), may hold values from -6 to 6
- adjoint: float32 [64, 4, 64, 1024], P('tm', None, 'space'), may hold values from -6 to 6
- source: float32 [64, 4, 64, 1024], P('tm', None, 'space'), may hold values from -6 to 6
- target: float32 [64, 4, 64, 1024], P('tm', None, 'space'), may hold values from -6 to 6
- conductivity: float32 [4, 64, 1024], P(None, 'space'), may hold values from 0.5 to 2
Outputs:
- new_state: float32 [64, 4, 64, 1024], P('tm', None, 'space')
- new_adjoint: float32 [64, 4, 64, 1024], P('tm', None, 'space')
All inputs are finite; a program needn't handle non-finite values.
Results may differ from a plain program's by a relative error of at most 0.0003.
Values sent between devices are 32-bit elements; how exact they have to be, the bound alone decides.
No kernel may reach another device: no remote copies, remote signals or barrier semaphores. Data moves between devices by JAX's collectives and lax.ppermute only.
A program may use at most 128 MiB of HBM per device.

v0:
```python
import math

import jax
import jax.numpy as jnp
from jax import lax
from jax.sharding import PartitionSpec as P

SWEEPS = 8


step_scale = 0.5
penalty = 0.05


def extended(cells, sides, width):
    for axis, dim in sides:
        count = lax.axis_size(axis)
        ends = count - 1
        head = lax.slice_in_dim(cells, 0, width, axis=dim)
        tail = lax.slice_in_dim(cells, cells.shape[dim] - width, cells.shape[dim], axis=dim)
        cells = jnp.concatenate(
            [
                lax.ppermute(tail, axis, [(i, (i + 1) % count) for i in range(ends)]),
                cells,
                lax.ppermute(head, axis, [((i + 1) % count, i) for i in range(ends)]),
            ],
            axis=dim,
        )
    return cells


def from_behind(block, axis, distance):
    devices = range(lax.axis_size(axis))
    route = [((i - distance) % len(devices), i) for i in devices]
    return lax.ppermute(block, axis, route)


def partner_2(shard, axis, bit):
    return lax.ppermute(shard, axis, [(i, i ^ 1 << bit) for i in range(lax.axis_size(axis))])


def faces(padded):
    return [
        padded[..., :-2, 1:-1, 1:-1],
        padded[..., 2:, 1:-1, 1:-1],
        padded[..., 1:-1, :-2, 1:-1],
        padded[..., 1:-1, 2:, 1:-1],
        padded[..., 1:-1, 1:-1, :-2],
        padded[..., 1:-1, 1:-1, 2:],
    ]


def pad_local(rimmed):
    widths = [(0, 0)] * (rimmed.ndim - 3) + [(1, 1), (0, 0), (1, 1)]
    return jnp.pad(rimmed, widths)


def neighbours(rimmed, weights):
    total = None
    for weight, near in zip(weights, faces(pad_local(rimmed))):
        term = weight * near
        total = term if total is None else total + term
    return total


def apply_split(rhs, a_first, a_second, big_b, inv_first, inv_second):
    coupling = step_scale / penalty
    ur, vr, ui, vi = (rhs[0], rhs[1], rhs[2], rhs[3])
    return jnp.stack(
        [
            (a_first * ur + big_b * ui - coupling * vr) * inv_first,
            (step_scale * ur + a_first * vr - big_b * vi) * inv_first,
            (a_second * ui - big_b * ur - coupling * vi) * inv_second,
            (step_scale * ui + a_second * vi + big_b * vr) * inv_second,
        ]
    )


def tables(count, sign):
    index = jnp.arange(count)
    angle = 2.0 * math.pi * (index[:, None] * index[None, :] % count).astype(jnp.float32) / count
    return (jnp.cos(angle), sign * jnp.sin(angle))


def mix(matrix, field):
    return jnp.einsum("kl,flprc->fkprc", matrix, field, precision=lax.Precision.HIGHEST)


def rotate(field, cosine, sine):
    real_part, imag_part = (field[:2], field[2:])
    return jnp.concatenate(
        [real_part * cosine - imag_part * sine, imag_part * cosine + real_part * sine], axis=0
    )


def body(state, adjoint, source, target, conductivity):
    local_steps = state.shape[0]
    tm_count = lax.axis_size("tm")
    bits = tm_count.bit_length() - 1
    period = local_steps * tm_count
    device = lax.axis_index("tm")
    kappa_rim = extended(conductivity, (("space", 1),), 1)
    weights = [0.5 * (conductivity + near) for near in faces(pad_local(kappa_rim))]
    diag = weights[0]
    for weight in weights[1:]:
        diag = diag + weight
    both = jnp.stack([state, adjoint])
    both_rim = extended(both, (("space", 3),), 1)
    near_both = neighbours(both_rim, weights)
    prior = from_behind(state[-1:], "tm", 1)
    later = from_behind(adjoint[:1], "tm", -1)
    state_prev = jnp.concatenate([prior, state[:-1]], axis=0)
    adjoint_next = jnp.concatenate([adjoint[1:], later], axis=0)
    k_state = diag * state - near_both[0]
    k_adjoint = diag * adjoint - near_both[1]
    state_res = step_scale * source - (
        state - state_prev + step_scale * k_state + step_scale / penalty * adjoint
    )
    adjoint_res = -step_scale * target - (
        adjoint - adjoint_next + step_scale * k_adjoint - step_scale * state
    )
    residual = jnp.stack([state_res, adjoint_res])
    slots = jnp.arange(local_steps)
    reversed_index = jnp.zeros((), jnp.int32)
    for digit in range(bits):
        reversed_index = reversed_index + device // 2**digit % 2 * 2 ** (bits - 1 - digit)

    def section_terms(digit):
        half = 2**digit
        lower = device // half % 2 == 0
        phase = 2.0 * math.pi * (device % half).astype(jnp.float32) / (2 * half)
        return (lower, jnp.cos(phase), jnp.sin(phase))

    lower, cosine, sine = section_terms(bits - 1)
    partner = partner_2(residual, "tm", bits - 1)
    apart = partner - residual
    spectrum = jnp.concatenate(
        [
            jnp.where(lower, residual + partner, apart * cosine),
            jnp.where(lower, 0.0, -apart * sine),
        ],
        axis=0,
    )
    for digit in range(bits - 2, -1, -1):
        lower, cosine, sine = section_terms(digit)
        partner = partner_2(spectrum, "tm", digit)
        apart = partner - spectrum
        spectrum = jnp.where(lower, spectrum + partner, rotate(apart, cosine, -sine))
    twist = 2.0 * math.pi * (slots * reversed_index % period).astype(jnp.float32) / period
    twist_cos = jnp.cos(twist)[None, :, None, None, None]
    twist_sin = jnp.sin(twist)[None, :, None, None, None]
    spectrum = rotate(spectrum, twist_cos, -twist_sin)
    cos_local, sin_local = tables(local_steps, -1.0)
    spectrum = jnp.concatenate(
        [
            mix(cos_local, spectrum[:2]) - mix(sin_local, spectrum[2:]),
            mix(cos_local, spectrum[2:]) + mix(sin_local, spectrum[:2]),
        ],
        axis=0,
    )
    freq = reversed_index + tm_count * slots
    first_angle = 2.0 * math.pi * (freq % period).astype(jnp.float32) / period
    a_first = (1.0 - jnp.cos(first_angle))[:, None, None, None] + step_scale * diag
    big_b = jnp.sin(first_angle)[:, None, None, None]
    inv_first = 1.0 / (a_first * a_first + big_b * big_b + step_scale * step_scale / penalty)
    guess = apply_split(spectrum, a_first, a_first, big_b, inv_first, inv_first)
    for sweep in range(SWEEPS - 1):
        guess_rim = extended(guess, (("space", 3),), 1)
        guess = apply_split(
            spectrum + step_scale * neighbours(guess_rim, weights),
            a_first,
            a_first,
            big_b,
            inv_first,
            inv_first,
        )
    cos_local, sin_local = tables(local_steps, 1.0)
    values = (
        jnp.concatenate(
            [
                mix(cos_local, guess[:2]) - mix(sin_local, guess[2:]),
                mix(cos_local, guess[2:]) + mix(sin_local, guess[:2]),
            ],
            axis=0,
        )
        / local_steps
    )
    values = rotate(values, twist_cos, twist_sin)
    for digit in range(0, bits - 1):
        lower, cosine, sine = section_terms(digit)
        sending = jnp.where(lower, values, rotate(values, cosine, sine))
        partner = partner_2(sending, "tm", digit)
        values = jnp.where(lower, (sending + partner) * 0.5, (partner - sending) * 0.5)
    lower, cosine, sine = section_terms(bits - 1)
    sending = jnp.where(lower, values[:2], values[:2] * cosine - values[2:] * sine)
    partner = partner_2(sending, "tm", bits - 1)
    correction = jnp.where(lower, (sending + partner) * 0.5, (partner - sending) * 0.5)
    return (state + correction[0], adjoint + correction[1])


def solution(mesh):
    return jax.shard_map(
        body,
        mesh=mesh,
        in_specs=(
            P("tm", None, "space", None),
            P("tm", None, "space", None),
            P("tm", None, "space", None),
            P("tm", None, "space", None),
            P(None, "space", None),
        ),
        out_specs=(P("tm", None, "space", None), P("tm", None, "space", None)),
        check_vma=False,
    )
```

profile of v0, /device:TPU:2, one launch (start us, length us, event | category | flops | bytes accessed | tf_op | source)
XLA Modules:
  0.0 471.7 jit_solution(4200782283451096903)
XLA Ops:
  6.1 4.4 collective-permute-start.3
  15.8 4.0 collective-permute-start.5
  23.9 2.5 collective-permute-start.6
  26.5 12.6 %collective-permute-done.6 = f32[2,2,4,8,1024]{4,3,2,1,0:T(8,128)S(1)} collective-permute-done((f32[2,2,4,8,1024]{4,3,2,1,0:T(8,128)S(1)}, f32[2,2,4,8,1024]{4,3,2,1,0:T(8,128)S(1)}, u32[]{:S(2)}, u32[]{:S(2)}) %collective-permute-start.6) | collective-permute-done | bytes 524320 | tf_op jit(solution)/shard_map/ppermute | solution.py:39
  40.4 2.8 collective-permute-start.7
  43.4 23.8 %collective-permute-done.7 = f32[4,2,4,8,1024]{4,3,2,1,0:T(8,128)S(1)} collective-permute-done((f32[4,2,4,8,1024]{4,3,2,1,0:T(8,128)}, f32[4,2,4,8,1024]{4,3,2,1,0:T(8,128)S(1)}, u32[]{:S(2)}, u32[]{:S(2)}) %collective-permute-start.7) | collective-permute-done | bytes 1048608 | tf_op jit(solution)/shard_map/ppermute | solution.py:39
  69.7 4.2 collective-permute-start.8
  74.0 47.6 %collective-permute-done.8 = f32[4,2,4,8,1024]{4,3,2,1,0:T(8,128)S(1)} collective-permute-done((f32[4,2,4,8,1024]{4,3,2,1,0:T(8,128)S(1)}, f32[4,2,4,8,1024]{4,3,2,1,0:T(8,128)S(1)}, u32[]{:S(2)}, u32[]{:S(2)}) %collective-permute-start.8) | collective-permute-done | bytes 1048608 | tf_op jit(solution)/shard_map/ppermute | solution.py:39
  124.4 47.5 %collective-permute-done.9 = f32[4,2,4,8,1024]{4,3,2,1,0:T(8,128)S(1)} collective-permute-done((f32[4,2,4,8,1024]{4,3,2,1,0:T(8,128)S(1)}, f32[4,2,4,8,1024]{4,3,2,1,0:T(8,128)S(1)}, u32[]{:S(2)}, u32[]{:S(2)}) %collective-permute-start.9) | collective-permute-done | bytes 1048608 | tf_op jit(solution)/shard_map/ppermute | solution.py:39
  175.2 24.0 %collective-permute-done.10 = f32[4,2,4,8,1024]{4,3,2,1,0:T(8,128)S(1)} collective-permute-done((f32[4,2,4,8,1024]{4,3,2,1,0:T(8,128)S(1)}, f32[4,2,4,8,1024]{4,3,2,1,0:T(8,128)S(1)}, u32[]{:S(2)}, u32[]{:S(2)}) %collective-permute-start.10) | collective-permute-done | bytes 1048608 | tf_op jit(solution)/shard_map/ppermute | solution.py:39
  200.1 2.1 fusion.93
  214.2 2.2 select_maximum_fusion.30
  218.6 4.0 collective-permute-start.13
  225.9 2.2 select_maximum_fusion.25
  230.3 5.0 %collective-permute-start.15 = (f32[4,2,4,1,1024]{4,3,2,1,0:T(1,128)S(1)}, f32[4,2,4,1,1024]{4,3,2,1,0:T(1,128)S(1)}, u32[]{:S(2)}, u32[]{:S(2)}) collective-permute-start(f32[4,2,4,1,1024]{4,3,2,1,0:T(1,128)S(1)} %get-tuple-element.65), channel_id=1, source_target_pairs={{0,1},{1,2},{2,3},{3,4},{4,5},{5,6},{6,7},{8,9},{9,10},{10,11},{11... | collective-permute-start | bytes 393224 | tf_op jit(solution)/shard_map/ppermute | solution.py:23
  238.6 2.2 select_maximum_fusion.20
  243.0 5.0 %collective-permute-start.17 = (f32[4,2,4,1,1024]{4,3,2,1,0:T(1,128)S(1)}, f32[4,2,4,1,1024]{4,3,2,1,0:T(1,128)S(1)}, u32[]{:S(2)}, u32[]{:S(2)}) collective-permute-start(f32[4,2,4,1,1024]{4,3,2,1,0:T(1,128)S(1)} %get-tuple-element.63), channel_id=1, source_target_pairs={{0,1},{1,2},{2,3},{3,4},{4,5},{5,6},{6,7},{8,9},{9,10},{10,11},{11... | collective-permute-start | bytes 393224 | tf_op jit(solution)/shard_map/ppermute | solution.py:23
  251.2 2.2 select_maximum_fusion.15
  255.7 5.0 %collective-permute-start.19 = (f32[4,2,4,1,1024]{4,3,2,1,0:T(1,128)S(1)}, f32[4,2,4,1,1024]{4,3,2,1,0:T(1,128)S(1)}, u32[]{:S(2)}, u32[]{:S(2)}) collective-permute-start(f32[4,2,4,1,1024]{4,3,2,1,0:T(1,128)S(1)} %get-tuple-element.61), channel_id=1, source_target_pairs={{0,1},{1,2},{2,3},{3,4},{4,5},{5,6},{6,7},{8,9},{9,10},{10,11},{11... | collective-permute-start | bytes 393224 | tf_op jit(solution)/shard_map/ppermute | solution.py:23
  263.9 2.2 select_maximum_fusion.10
  268.4 5.0 %collective-permute-start.21 = (f32[4,2,4,1,1024]{4,3,2,1,0:T(1,128)S(1)}, f32[4,2,4,1,1024]{4,3,2,1,0:T(1,128)S(1)}, u32[]{:S(2)}, u32[]{:S(2)}) collective-permute-start(f32[4,2,4,1,1024]{4,3,2,1,0:T(1,128)S(1)} %get-tuple-element.59), channel_id=1, source_target_pairs={{0,1},{1,2},{2,3},{3,4},{4,5},{5,6},{6,7},{8,9},{9,10},{10,11},{11... | collective-permute-start | bytes 393224 | tf_op jit(solution)/shard_map/ppermute | solution.py:23
  276.6 2.2 select_maximum_fusion.5
  281.0 5.0 %collective-permute-start.23 = (f32[4,2,4,1,1024]{4,3,2,1,0:T(1,128)S(1)}, f32[4,2,4,1,1024]{4,3,2,1,0:T(1,128)S(1)}, u32[]{:S(2)}, u32[]{:S(2)}) collective-permute-start(f32[4,2,4,1,1024]{4,3,2,1,0:T(1,128)S(1)} %get-tuple-element.57), channel_id=1, source_target_pairs={{0,1},{1,2},{2,3},{3,4},{4,5},{5,6},{6,7},{8,9},{9,10},{10,11},{11... | collective-permute-start | bytes 393224 | tf_op jit(solution)/shard_map/ppermute | solution.py:23
  289.2 2.2 select_maximum_fusion
  303.9 23.5 %collective-permute-done.25 = f32[4,2,4,8,1024]{4,3,2,1,0:T(8,128)S(1)} collective-permute-done((f32[4,2,4,8,1024]{4,3,2,1,0:T(8,128)S(1)}, f32[4,2,4,8,1024]{4,3,2,1,0:T(8,128)S(1)}, u32[]{:S(2)}, u32[]{:S(2)}) %collective-permute-start.25) | collective-permute-done | bytes 1048608 | tf_op jit(solution)/shard_map/ppermute | solution.py:39
  327.9 2.3 collective-permute-start.26
  330.3 47.2 %collective-permute-done.26 = f32[4,2,4,8,1024]{4,3,2,1,0:T(8,128)S(1)} collective-permute-done((f32[4,2,4,8,1024]{4,3,2,1,0:T(8,128)S(1)}, f32[4,2,4,8,1024]{4,3,2,1,0:T(8,128)S(1)}, u32[]{:S(2)}, u32[]{:S(2)}) %collective-permute-start.26) | collective-permute-done | bytes 1048608 | tf_op jit(solution)/shard_map/ppermute | solution.py:39
  378.1 3.0 collective-permute-start.27
  381.1 48.4 %collective-permute-done.27 = f32[4,2,4,8,1024]{4,3,2,1,0:T(8,128)S(1)} collective-permute-done((f32[4,2,4,8,1024]{4,3,2,1,0:T(8,128)S(1)}, f32[4,2,4,8,1024]{4,3,2,1,0:T(8,128)S(1)}, u32[]{:S(2)}, u32[]{:S(2)}) %collective-permute-start.27) | collective-permute-done | bytes 1048608 | tf_op jit(solution)/shard_map/ppermute | solution.py:39
  431.3 24.0 %collective-permute-done.28 = f32[4,2,4,8,1024]{4,3,2,1,0:T(8,128)S(1)} collective-permute-done((f32[4,2,4,8,1024]{4,3,2,1,0:T(8,128)S(1)}, f32[4,2,4,8,1024]{4,3,2,1,0:T(8,128)S(1)}, u32[]{:S(2)}, u32[]{:S(2)}) %collective-permute-start.28) | collective-permute-done | bytes 1048608 | tf_op jit(solution)/shard_map/ppermute | solution.py:39
  455.6 2.2 collective-permute-start.29
  457.8 12.4 %collective-permute-done.29 = f32[2,2,4,8,1024]{4,3,2,1,0:T(8,128)S(1)} collective-permute-done((f32[2,2,4,8,1024]{4,3,2,1,0:T(8,128)S(1)}, f32[2,2,4,8,1024]{4,3,2,1,0:T(8,128)S(1)}, u32[]{:S(2)}, u32[]{:S(2)}) %collective-permute-start.29) | collective-permute-done | bytes 524320 | tf_op jit(solution)/shard_map/ppermute | solution.py:39
  (131 shorter events, 86.1 us)
Async XLA Ops:
  0.6 21.6 %copy-start.1 = (f32[2,4,8,1024]{3,2,1,0:T(8,128)S(1)}, f32[2,4,8,1024]{3,2,1,0:T(8,128)}, u32[]{:S(2)}) copy-start(f32[2,4,8,1024]{3,2,1,0:T(8,128)} %param.5) | copy-start | bytes 786436
  0.6 21.6 %copy-start = (f32[2,4,8,1024]{3,2,1,0:T(8,128)S(1)}, f32[2,4,8,1024]{3,2,1,0:T(8,128)}, u32[]{:S(2)}) copy-start(f32[2,4,8,1024]{3,2,1,0:T(8,128)} %param.6) | copy-start | bytes 786436
  1.7 14.1 %collective-permute-start = (f32[4,1,1024]{2,1,0:T(1,128)S(1)}, f32[4,1,1024]{2,1,0:T(1,128)S(1)}, u32[]{:S(2)}, u32[]{:S(2)}) collective-permute-start(f32[4,1,1024]{2,1,0:T(1,128)S(1)} %get-tuple-element.89), channel_id=1, source_target_pairs={{0,1},{1,2},{2,3},{3,4},{4,5},{5,6},{6,7},{8,9},{9,10},{10,11},{11... | collective-permute-start | bytes 49160 | tf_op jit(solution)/shard_map/ppermute | solution.py:23
  3.5 16.3 %collective-permute-start.1 = (f32[4,1,1024]{2,1,0:T(1,128)S(1)}, f32[4,1,1024]{2,1,0:T(1,128)S(1)}, u32[]{:S(2)}, u32[]{:S(2)}) collective-permute-start(f32[4,1,1024]{2,1,0:T(1,128)S(1)} %get-tuple-element.90), channel_id=1, source_target_pairs={{1,0},{2,1},{3,2},{4,3},{5,4},{6,5},{7,6},{9,8},{10,9},{11,10},{12... | collective-permute-start | bytes 49160 | tf_op jit(solution)/shard_map/ppermute | solution.py:25
  6.1 16.1 %collective-permute-start.3 = (f32[2,2,4,1,1024]{4,3,2,1,0:T(1,128)S(1)}, f32[2,2,4,1,1024]{4,3,2,1,0:T(1,128)S(1)}, u32[]{:S(2)}, u32[]{:S(2)}) collective-permute-start(f32[2,2,4,1,1024]{4,3,2,1,0:T(1,128)S(1)} %get-tuple-element.83), channel_id=1, source_target_pairs={{0,1},{1,2},{2,3},{3,4},{4,5},{5,6},{6,7},{8,9},{9,10},{10,11},{11... | collective-permute-start | bytes 196616 | tf_op jit(solution)/shard_map/ppermute | solution.py:23
  10.5 11.7 %collective-permute-start.4 = (f32[2,2,4,1,1024]{4,3,2,1,0:T(1,128)S(1)}, f32[2,2,4,1,1024]{4,3,2,1,0:T(1,128)S(1)}, u32[]{:S(2)}, u32[]{:S(2)}) collective-permute-start(f32[2,2,4,1,1024]{4,3,2,1,0:T(1,128)S(1)} %get-tuple-element.84), channel_id=1, source_target_pairs={{1,0},{2,1},{3,2},{4,3},{5,4},{6,5},{7,6},{9,8},{10,9},{11,10},{12... | collective-permute-start | bytes 196616 | tf_op jit(solution)/shard_map/ppermute | solution.py:25
  12.8 10.8 %collective-permute-start.2 = (f32[1,4,8,1024]{3,2,1,0:T(8,128)S(1)}, f32[1,4,8,1024]{3,2,1,0:T(8,128)S(1)}, u32[]{:S(2)}, u32[]{:S(2)}) collective-permute-start(f32[1,4,8,1024]{3,2,1,0:T(8,128)S(1)} %get-tuple-element.85), channel_id=1, source_target_pairs={{248,0},{0,8},{8,16},{16,24},{24,32},{32,40},{40,48},{48,56},{56,6... | collective-permute-start | bytes 393224 | tf_op jit(solution)/shard_map/ppermute | solution.py:35
  15.8 7.8 %collective-permute-start.5 = (f32[1,4,8,1024]{3,2,1,0:T(8,128)S(1)}, f32[1,4,8,1024]{3,2,1,0:T(8,128)S(1)}, u32[]{:S(2)}, u32[]{:S(2)}) collective-permute-start(f32[1,4,8,1024]{3,2,1,0:T(8,128)S(1)} %get-tuple-element.88), channel_id=1, source_target_pairs={{8,0},{16,8},{24,16},{32,24},{40,32},{48,40},{56,48},{64,56},{72,6... | collective-permute-start | bytes 393224 | tf_op jit(solution)/shard_map/ppermute | solution.py:35
  23.9 15.3 %collective-permute-start.6 = (f32[2,2,4,8,1024]{4,3,2,1,0:T(8,128)S(1)}, f32[2,2,4,8,1024]{4,3,2,1,0:T(8,128)S(1)}, u32[]{:S(2)}, u32[]{:S(2)}) collective-permute-start(f32[2,2,4,8,1024]{4,3,2,1,0:T(8,128)S(1)} %pad_maximum_fusion.62), channel_id=1, source_target_pairs={{0,128},{8,136},{16,144},{24,152},{32,160},{40,168},{48,176},{56,1... | collective-permute-start | bytes 1572872 | tf_op jit(solution)/shard_map/ppermute | solution.py:39
  40.4 26.7 %collective-permute-start.7 = (f32[4,2,4,8,1024]{4,3,2,1,0:T(8,128)}, f32[4,2,4,8,1024]{4,3,2,1,0:T(8,128)S(1)}, u32[]{:S(2)}, u32[]{:S(2)}) collective-permute-start(f32[4,2,4,8,1024]{4,3,2,1,0:T(8,128)} %pad_maximum_fusion.56), channel_id=1, source_target_pairs={{0,64},{8,72},{16,80},{24,88},{32,96},{40,104},{48,112},{56,120},{... | collective-permute-start | bytes 3145736 | tf_op jit(solution)/shard_map/ppermute | solution.py:39
  69.7 51.9 %collective-permute-start.8 = (f32[4,2,4,8,1024]{4,3,2,1,0:T(8,128)S(1)}, f32[4,2,4,8,1024]{4,3,2,1,0:T(8,128)S(1)}, u32[]{:S(2)}, u32[]{:S(2)}) collective-permute-start(f32[4,2,4,8,1024]{4,3,2,1,0:T(8,128)S(1)} %maximum_select_fusion), channel_id=1, source_target_pairs={{0,32},{8,40},{16,48},{24,56},{32,0},{40,8},{48,16},{56,24},{64,96... | collective-permute-start | bytes 3145736 | tf_op jit(solution)/shard_map/ppermute | solution.py:39
  124.1 47.7 %collective-permute-start.9 = (f32[4,2,4,8,1024]{4,3,2,1,0:T(8,128)S(1)}, f32[4,2,4,8,1024]{4,3,2,1,0:T(8,128)S(1)}, u32[]{:S(2)}, u32[]{:S(2)}) collective-permute-start(f32[4,2,4,8,1024]{4,3,2,1,0:T(8,128)S(1)} %maximum_select_fusion.1), channel_id=1, source_target_pairs={{0,16},{8,24},{16,0},{24,8},{32,48},{40,56},{48,32},{56,40},{64,80... | collective-permute-start | bytes 3145736 | tf_op jit(solution)/shard_map/ppermute | solution.py:39
  174.4 24.8 %collective-permute-start.10 = (f32[4,2,4,8,1024]{4,3,2,1,0:T(8,128)S(1)}, f32[4,2,4,8,1024]{4,3,2,1,0:T(8,128)S(1)}, u32[]{:S(2)}, u32[]{:S(2)}) collective-permute-start(f32[4,2,4,8,1024]{4,3,2,1,0:T(8,128)S(1)} %maximum_select_fusion.2), channel_id=1, source_target_pairs={{0,8},{8,0},{16,24},{24,16},{32,40},{40,32},{48,56},{56,48},{64,72... | collective-permute-start | bytes 3145736 | tf_op jit(solution)/shard_map/ppermute | solution.py:39
  209.6 2.8 collective-permute-start.11
  210.9 3.2 collective-permute-start.12
  218.6 5.3 %collective-permute-start.13 = (f32[4,2,4,1,1024]{4,3,2,1,0:T(1,128)S(1)}, f32[4,2,4,1,1024]{4,3,2,1,0:T(1,128)S(1)}, u32[]{:S(2)}, u32[]{:S(2)}) collective-permute-start(f32[4,2,4,1,1024]{4,3,2,1,0:T(1,128)S(1)} %get-tuple-element.67), channel_id=1, source_target_pairs={{0,1},{1,2},{2,3},{3,4},{4,5},{5,6},{6,7},{8,9},{9,10},{10,11},{11... | collective-permute-start | bytes 393224 | tf_op jit(solution)/shard_map/ppermute | solution.py:23
  222.7 3.2 collective-permute-start.14
  230.3 6.3 %collective-permute-start.15 = (f32[4,2,4,1,1024]{4,3,2,1,0:T(1,128)S(1)}, f32[4,2,4,1,1024]{4,3,2,1,0:T(1,128)S(1)}, u32[]{:S(2)}, u32[]{:S(2)}) collective-permute-start(f32[4,2,4,1,1024]{4,3,2,1,0:T(1,128)S(1)} %get-tuple-element.65), channel_id=1, source_target_pairs={{0,1},{1,2},{2,3},{3,4},{4,5},{5,6},{6,7},{8,9},{9,10},{10,11},{11... | collective-permute-start | bytes 393224 | tf_op jit(solution)/shard_map/ppermute | solution.py:23
  235.3 3.2 collective-permute-start.16
  243.0 6.3 %collective-permute-start.17 = (f32[4,2,4,1,1024]{4,3,2,1,0:T(1,128)S(1)}, f32[4,2,4,1,1024]{4,3,2,1,0:T(1,128)S(1)}, u32[]{:S(2)}, u32[]{:S(2)}) collective-permute-start(f32[4,2,4,1,1024]{4,3,2,1,0:T(1,128)S(1)} %get-tuple-element.63), channel_id=1, source_target_pairs={{0,1},{1,2},{2,3},{3,4},{4,5},{5,6},{6,7},{8,9},{9,10},{10,11},{11... | collective-permute-start | bytes 393224 | tf_op jit(solution)/shard_map/ppermute | solution.py:23
  248.0 3.2 collective-permute-start.18
  255.7 6.5 %collective-permute-start.19 = (f32[4,2,4,1,1024]{4,3,2,1,0:T(1,128)S(1)}, f32[4,2,4,1,1024]{4,3,2,1,0:T(1,128)S(1)}, u32[]{:S(2)}, u32[]{:S(2)}) collective-permute-start(f32[4,2,4,1,1024]{4,3,2,1,0:T(1,128)S(1)} %get-tuple-element.61), channel_id=1, source_target_pairs={{0,1},{1,2},{2,3},{3,4},{4,5},{5,6},{6,7},{8,9},{9,10},{10,11},{11... | collective-permute-start | bytes 393224 | tf_op jit(solution)/shard_map/ppermute | solution.py:23
  260.7 3.2 collective-permute-start.20
  268.4 6.3 %collective-permute-start.21 = (f32[4,2,4,1,1024]{4,3,2,1,0:T(1,128)S(1)}, f32[4,2,4,1,1024]{4,3,2,1,0:T(1,128)S(1)}, u32[]{:S(2)}, u32[]{:S(2)}) collective-permute-start(f32[4,2,4,1,1024]{4,3,2,1,0:T(1,128)S(1)} %get-tuple-element.59), channel_id=1, source_target_pairs={{0,1},{1,2},{2,3},{3,4},{4,5},{5,6},{6,7},{8,9},{9,10},{10,11},{11... | collective-permute-start | bytes 393224 | tf_op jit(solution)/shard_map/ppermute | solution.py:23
  273.3 3.2 collective-permute-start.22
  281.0 6.3 %collective-permute-start.23 = (f32[4,2,4,1,1024]{4,3,2,1,0:T(1,128)S(1)}, f32[4,2,4,1,1024]{4,3,2,1,0:T(1,128)S(1)}, u32[]{:S(2)}, u32[]{:S(2)}) collective-permute-start(f32[4,2,4,1,1024]{4,3,2,1,0:T(1,128)S(1)} %get-tuple-element.57), channel_id=1, source_target_pairs={{0,1},{1,2},{2,3},{3,4},{4,5},{5,6},{6,7},{8,9},{9,10},{10,11},{11... | collective-permute-start | bytes 393224 | tf_op jit(solution)/shard_map/ppermute | solution.py:23
  286.0 3.2 collective-permute-start.24
  303.4 24.0 %collective-permute-start.25 = (f32[4,2,4,8,1024]{4,3,2,1,0:T(8,128)S(1)}, f32[4,2,4,8,1024]{4,3,2,1,0:T(8,128)S(1)}, u32[]{:S(2)}, u32[]{:S(2)}) collective-permute-start(f32[4,2,4,8,1024]{4,3,2,1,0:T(8,128)S(1)} %maximum_select_fusion.4), channel_id=1, source_target_pairs={{0,8},{8,0},{16,24},{24,16},{32,40},{40,32},{48,56},{56,48},{64,72... | collective-permute-start | bytes 3145736 | tf_op jit(solution)/shard_map/ppermute | solution.py:39
  327.9 49.6 %collective-permute-start.26 = (f32[4,2,4,8,1024]{4,3,2,1,0:T(8,128)S(1)}, f32[4,2,4,8,1024]{4,3,2,1,0:T(8,128)S(1)}, u32[]{:S(2)}, u32[]{:S(2)}) collective-permute-start(f32[4,2,4,8,1024]{4,3,2,1,0:T(8,128)S(1)} %maximum_select_fusion.5), channel_id=1, source_target_pairs={{0,16},{8,24},{16,0},{24,8},{32,48},{40,56},{48,32},{56,40},{64,80... | collective-permute-start | bytes 3145736 | tf_op jit(solution)/shard_map/ppermute | solution.py:39
  378.1 51.4 %collective-permute-start.27 = (f32[4,2,4,8,1024]{4,3,2,1,0:T(8,128)S(1)}, f32[4,2,4,8,1024]{4,3,2,1,0:T(8,128)S(1)}, u32[]{:S(2)}, u32[]{:S(2)}) collective-permute-start(f32[4,2,4,8,1024]{4,3,2,1,0:T(8,128)S(1)} %maximum_select_fusion.6), channel_id=1, source_target_pairs={{0,32},{8,40},{16,48},{24,56},{32,0},{40,8},{48,16},{56,24},{64,96... | collective-permute-start | bytes 3145736 | tf_op jit(solution)/shard_map/ppermute | solution.py:39
  430.1 25.2 %collective-permute-start.28 = (f32[4,2,4,8,1024]{4,3,2,1,0:T(8,128)S(1)}, f32[4,2,4,8,1024]{4,3,2,1,0:T(8,128)S(1)}, u32[]{:S(2)}, u32[]{:S(2)}) collective-permute-start(f32[4,2,4,8,1024]{4,3,2,1,0:T(8,128)S(1)} %maximum_select_fusion.7), channel_id=1, source_target_pairs={{0,64},{8,72},{16,80},{24,88},{32,96},{40,104},{48,112},{56,120},{... | collective-permute-start | bytes 3145736 | tf_op jit(solution)/shard_map/ppermute | solution.py:39
  455.6 14.6 %collective-permute-start.29 = (f32[2,2,4,8,1024]{4,3,2,1,0:T(8,128)S(1)}, f32[2,2,4,8,1024]{4,3,2,1,0:T(8,128)S(1)}, u32[]{:S(2)}, u32[]{:S(2)}) collective-permute-start(f32[2,2,4,8,1024]{4,3,2,1,0:T(8,128)S(1)} %fusion.70), channel_id=1, source_target_pairs={{0,128},{8,136},{16,144},{24,152},{32,160},{40,168},{48,176},{56,1... | collective-permute-start | bytes 1572872 | tf_op jit(solution)/shard_map/ppermute | solution.py:39
  (5 other events, 5.9 us)
where the time goes:
time: 479 us; the launch traced here: 472 us
  waiting for transfers between devices  324 us (68%)
  starting transfers between devices  73.7 us (15%)
  other arithmetic  49.2 us (10%)
  matrix products  16.8 us (4%)
  local copies, waits for them, and re-layouts  5.21 us (1%)
    ppermute x10, waiting for transfers between devices, partner_2(): lax.ppermute(shard, axis, [(i, i ^ 1 << bit) for i in range(lax.axis_size...  311 us
    ppermute x9, starting transfers between devices, extended(): lax.ppermute(tail, axis, [(i, (i + 1) % count) for i in range(ends)])  36.3 us
    ppermute x10, starting transfers between devices, partner_2(): lax.ppermute(shard, axis, [(i, i ^ 1 << bit) for i in range(lax.axis_size...  19.4 us
    concatenate x9, other arithmetic, extended(): jnp.concatenate([lax.ppermute(tail, axis, [(i, (i + 1) % count) for i in...  17.4 us
    dot_general x8, matrix products, mix(): jnp.einsum('kl,flprc->fkprc', matrix, field, precision=lax.Precision.HIGH...  16.8 us
    ppermute x9, waiting for transfers between devices, extended(): lax.ppermute(head, axis, [((i + 1) % count, i) for i in range(ends)])  13.1 us
    ppermute x9, starting transfers between devices, extended(): lax.ppermute(head, axis, [((i + 1) % count, i) for i in range(ends)])  12 us
    add x7, other arithmetic, body(): spectrum + step_scale * neighbours(guess_rim, weights)  12 us
  transfers between devices with their start and end apart: 30, of which 17 were waited for; matrix products, arithmetic and copies ran while one was open for 2% of the time, Pallas kernels for 0%

commit v1 on v0

v1 whole, which is shorter than its diff:
```python
import functools
import math

import jax
import jax.numpy as jnp
import ml_dtypes
import numpy as np
from jax import lax
from jax.experimental import pallas as pl
from jax.experimental.pallas import tpu as pltpu
from jax.sharding import PartitionSpec as P

SWEEPS = 8
STEP = 0.5
PENALTY = 0.05
LANES = 128
WIDE = 8
DEEP = SWEEPS - 1
VMEM_LIMIT = 56 * 1024 * 1024


def transforms(period):
    q = STEP / PENALTY
    time = np.arange(period)
    pairs = [(0, 1)] + [(k, s) for k in range(1, period // 2) for s in (1, -1)] + [(period // 2, 1)]
    count = len(pairs)
    forward = np.zeros((period, 2, 2 * count))
    inverse = np.zeros((2 * count, period, 2))
    real_shift, imag_shift = np.zeros(count), np.zeros(count)
    for m, (k, sign) in enumerate(pairs):
        theta = 2.0 * math.pi * k / period
        sine = 0.0 if k in (0, period // 2) else math.sin(theta)
        root = math.sqrt(sine * sine + STEP * q)
        real_shift[m] = 1.0 - math.cos(theta)
        imag_shift[m] = sign * root
        wave = np.exp(-1j * theta * time)
        first = (root + sign * sine) / (2.0 * q * root) * wave
        second = -sign * 1j / (2.0 * root) * wave
        for f, row in enumerate((first, second)):
            forward[:, f, m] = row.real
            forward[:, f, count + m] = row.imag
        weight = 2.0 / period
        back = np.conj(wave) * weight
        for f, factor in enumerate((q, sign * 1j * (root - sign * sine))):
            inverse[m, :, f] = (factor * back).real
            inverse[count + m, :, f] = -(factor * back).imag
    real_lane = np.concatenate([real_shift, real_shift])
    imag_lane = np.concatenate([imag_shift, -imag_shift])
    return forward, inverse, np.stack([real_lane, imag_lane]).astype(np.float32)


def split_const(matrix):
    high = matrix.astype(np.float32).astype(ml_dtypes.bfloat16)
    low = (matrix - high.astype(np.float64)).astype(np.float32).astype(ml_dtypes.bfloat16)
    return high, low


def dot_split(left, high_ref, low_ref):
    high = left.astype(jnp.bfloat16)
    low = (left - high.astype(jnp.float32)).astype(jnp.bfloat16)
    dot = functools.partial(jnp.dot, preferred_element_type=jnp.float32)
    return dot(high, high_ref[...]) + (dot(low, high_ref[...]) + dot(high, low_ref[...]))


def residual_kernel(blocks, state, adjoint, source, target, prior, later, top, bottom, cond, out, res, turned):
    steps, planes, rows, cols = state.shape
    row = lax.broadcasted_iota(jnp.int32, (rows, cols), 0)
    col = lax.broadcasted_iota(jnp.int32, (rows, cols), 1)

    def near(value, above, below):
        up = jnp.where(row == 0, above, pltpu.roll(value, 1, axis=0))
        down = jnp.where(row == rows - 1, below, pltpu.roll(value, rows - 1, axis=0))
        left = jnp.where(col == 0, 0.0, pltpu.roll(value, 1, axis=1))
        right = jnp.where(col == cols - 1, 0.0, pltpu.roll(value, cols - 1, axis=1))
        return up, down, left, right

    edge = 2 * steps * planes
    kappa = [cond[p] for p in range(planes)]
    zero = jnp.zeros((rows, cols), jnp.float32)
    for p in range(planes):
        around = near(kappa[p], top[pl.ds(edge + p, 1)], bottom[pl.ds(edge + p, 1)])
        around += (kappa[p - 1] if p else zero, kappa[p + 1] if p < planes - 1 else zero)
        weights = [(0.5 * STEP) * (kappa[p] + k) for k in around]
        diag = weights[0]
        for w in weights[1:]:
            diag = diag + w
        for t in range(steps):
            stiff = []
            for f, field in enumerate((state, adjoint)):
                at = (f * steps + t) * planes + p
                value = field[t, p]
                sides = near(value, top[pl.ds(at, 1)], bottom[pl.ds(at, 1)])
                total = diag * value
                for w, v in zip(weights, sides):
                    total = total - w * v
                if p:
                    total = total - weights[4] * field[t, p - 1]
                if p < planes - 1:
                    total = total - weights[5] * field[t, p + 1]
                stiff.append(total)
            s, a = state[t, p], adjoint[t, p]
            before = state[t - 1, p] if t else prior[p]
            after = adjoint[t + 1, p] if t < steps - 1 else later[p]
            first = STEP * source[t, p] - (s - before + stiff[0] + (STEP / PENALTY) * a)
            second = -STEP * target[t, p] - (a - after + stiff[1] - STEP * s)
            for f, value in enumerate((first, second)):
                res[pl.ds(((t * 2 + f) * planes + p) * rows, rows), :] = value
    turned[pl.ds(0, WIDE), :] = jnp.zeros((WIDE, LANES), jnp.float32)
    turned[pl.ds(WIDE + cols, WIDE), :] = jnp.zeros((WIDE, LANES), jnp.float32)
    for tile in range(cols // LANES):
        turned[pl.ds(WIDE + tile * LANES, LANES), :] = res[:, pl.ds(tile * LANES, LANES)].T
    own = cols // blocks
    for j in range(blocks):
        out[j] = turned[pl.ds(j * own, own + 2 * WIDE), :]


def forward_kernel(shape, got, high, low, own, up, down, left):
    blocks, span, planes, rows = shape
    half = span // 2
    cells = planes * rows
    for g in range(span // 4):
        parts = [got[pl.ds(4 * g + c, blocks, stride=span), :] for c in range(4)]
        turned = jnp.concatenate(parts, axis=0).T
        for tf in range(4):
            left[pl.ds(g * cells, cells), pl.ds(tf * LANES, LANES)] = turned[tf * cells : (tf + 1) * cells]
    spectrum = dot_split(left[...], high, low)
    for g in range(span // 4):
        for c in range(4):
            side, at = divmod(4 * g + c, half)
            for p in range(planes):
                piece = spectrum[g * cells + p * rows : g * cells + (p + 1) * rows, c * LANES : (c + 1) * LANES]
                own[pl.ds(at * 2 * planes + side * planes + p, rows, stride=half * 2 * planes), :] = piece
    size = half * 2 * planes * DEEP
    up[...] = own[pl.ds(0, size), :]
    down[...] = own[pl.ds(half * 2 * planes, size), :]


def sweep_kernel(shape, own, above, below, kappa, shifts, high, low, out, rhs, first, second, w_row, w_col, w_plane, w_back, scale, cross, left):
    blocks, half, planes, rows = shape
    tall = rows + 2 * DEEP
    depth = 2 * planes
    block = (half, depth, LANES)

    position = lax.broadcasted_iota(jnp.int32, block, 1) % planes

    def beside(value):
        before = jnp.concatenate([pltpu.roll(value[half - 1], planes, axis=0)[None], value[:-1]], axis=0)
        after = jnp.concatenate([value[1:], pltpu.roll(value[0], planes, axis=0)[None]], axis=0)
        return before, after

    def bond(a, b):
        return jnp.where(a * b > 0.0, (0.5 * STEP) * (a + b), 0.0)

    side = lax.broadcasted_iota(jnp.int32, (half, depth, LANES), 1) // planes
    column = lax.broadcasted_iota(jnp.int32, (half, depth, LANES), 0)
    real = shifts[0:1, :][None]
    imag = shifts[1:2, :][None]

    def setup(r, _):
        k = kappa[r + 1]
        k_up, k_down = kappa[r], kappa[r + 2]
        k_left, k_right = beside(k)
        k_left = jnp.where((column == 0) & (side == 0), 0.0, k_left)
        k_right = jnp.where((column == half - 1) & (side == 1), 0.0, k_right)
        k_back = jnp.where(position == 0, 0.0, pltpu.roll(k, 1, axis=1))
        k_front = jnp.where(position == planes - 1, 0.0, pltpu.roll(k, depth - 1, axis=1))
        w_row[r] = bond(k, k_down)
        w_col[r] = bond(k, k_right)
        w_plane[r] = bond(k, k_front)
        w_back[r] = bond(k, k_back)
        big = (0.5 * STEP) * (6.0 * k + (k_up + k_down + k_left + k_right + k_back + k_front)) + real
        inv = 1.0 / (big * big + imag * imag)
        scale[r] = big * inv
        cross[r] = imag * inv

    lax.fori_loop(0, tall, setup, None)

    rhs[pl.ds(0, DEEP)] = above[...]
    rhs[pl.ds(DEEP, rows)] = own[...]
    rhs[pl.ds(DEEP + rows, DEEP)] = below[...]

    def solve(total, r):
        return scale[r] * total + cross[r] * pltpu.roll(total, LANES // 2, axis=2)

    def start(r, _):
        first[r] = solve(rhs[r], r)

    lax.fori_loop(0, tall, start, None)
    old, new = first, second
    for sweep in range(1, SWEEPS):

        def step(r, _, old=old, new=new):
            value = old[r]
            before, after = beside(value)
            weight = w_col[r]
            weight_before, _ = beside(weight)
            total = rhs[r] + weight * after + weight_before * before
            total = total + w_row[r] * old[r + 1] + w_row[r - 1] * old[r - 1]
            total = total + w_plane[r] * pltpu.roll(value, depth - 1, axis=1)
            total = total + w_back[r] * pltpu.roll(value, 1, axis=1)
            new[r] = solve(total, r)

        lax.fori_loop(sweep, tall - sweep, step, None)
        old, new = new, old

    cells = planes * rows
    own_cols = 2 * half - 2 * WIDE
    for g in range(own_cols // 4):
        for c in range(4):
            side_at, at = divmod(4 * g + c + WIDE, half)
            for p in range(planes):
                piece = old[pl.ds(DEEP, rows), at, side_at * planes + p, :]
                left[pl.ds(g * cells + p * rows, rows), pl.ds(c * LANES, LANES)] = piece
    values = dot_split(left[...], high, low)
    for g in range(own_cols // 4):
        parts = [values[g * cells : (g + 1) * cells, tf * LANES : (tf + 1) * LANES] for tf in range(4)]
        turned = jnp.concatenate(parts, axis=0).T
        for c in range(4):
            out[pl.ds(4 * g + c, blocks, stride=own_cols), :] = turned[c * blocks : (c + 1) * blocks]


def update_kernel(got, state, adjoint, new_state, new_adjoint):
    steps, planes, rows, cols = state.shape
    for tile in range(cols // LANES):
        block = got[pl.ds(tile * LANES, LANES), :].T
        for t in range(steps):
            for f, (old, new) in enumerate(((state, new_state), (adjoint, new_adjoint))):
                for p in range(planes):
                    at = ((t * 2 + f) * planes + p) * rows
                    new[t, p, :, pl.ds(tile * LANES, LANES)] = (
                        old[t, p, :, pl.ds(tile * LANES, LANES)] + block[at : at + rows]
                    )


def call(kernel, outs, scratch, flops, moved, *args):
    single = not isinstance(outs, list)
    return pl.pallas_call(
        kernel,
        out_shape=outs,
        in_specs=[pl.BlockSpec(memory_space=pltpu.VMEM)] * len(args),
        out_specs=pl.BlockSpec(memory_space=pltpu.VMEM) if single else [pl.BlockSpec(memory_space=pltpu.VMEM)] * len(outs),
        scratch_shapes=scratch,
        compiler_params=pltpu.CompilerParams(vmem_limit_bytes=VMEM_LIMIT),
        cost_estimate=pl.CostEstimate(flops=flops, bytes_accessed=moved, transcendentals=0),
    )(*args)


def f32(*shape):
    return jax.ShapeDtypeStruct(shape, jnp.float32)


def shift(block, axis, distance, wrap):
    count = lax.axis_size(axis)
    route = [(i, (i + distance) % count) for i in range(count) if wrap or 0 <= i + distance < count]
    return lax.ppermute(block, axis, route)


def body(state, adjoint, source, target, conductivity):
    steps, planes, rows, cols = state.shape
    blocks = lax.axis_size("tm")
    me = lax.axis_index("tm")
    own_cols = cols // blocks
    span = own_cols + 2 * WIDE
    half = span // 2
    depth = 2 * planes

    forward, inverse, shifts = transforms(steps * blocks)
    forward = forward.reshape(blocks, steps * 2, LANES).transpose(1, 0, 2)
    wide_forward = np.einsum("tis,cd->tcids", forward, np.eye(4)).reshape(4 * LANES, 4 * LANES)
    inverse = inverse.reshape(LANES, blocks, steps * 2).transpose(0, 2, 1)
    wide_inverse = np.einsum("sti,cd->cstdi", inverse, np.eye(4)).reshape(4 * LANES, 4 * LANES)
    forward_high, forward_low = split_const(wide_forward)
    inverse_high, inverse_low = split_const(wide_inverse)

    padded = jnp.pad(conductivity, ((0, 0), (0, 0), (WIDE, WIDE)))
    slab = lax.dynamic_slice(padded, (0, 0, me * own_cols), (planes, rows, span))
    slab_rows = jnp.pad(slab, ((0, 0), (0, 0), (0, LANES - span))).reshape(planes * rows * LANES // cols, cols)

    def edge(r):
        both = jnp.stack([state[:, :, r], adjoint[:, :, r]]).reshape(2 * steps * planes, cols)
        return jnp.concatenate([both, conductivity[:, r], slab_rows], axis=0)

    top = shift(edge(rows - 1), "space", 1, False)
    bottom = shift(edge(0), "space", -1, False)
    prior = shift(state[-1], "tm", 1, True)
    later = shift(adjoint[0], "tm", -1, True)

    sent = call(
        functools.partial(residual_kernel, blocks),
        f32(blocks, span, LANES),
        [pltpu.VMEM((LANES, cols), jnp.float32), pltpu.VMEM((cols + 2 * WIDE, LANES), jnp.float32)],
        10**7,
        3 * 10**6,
        state, adjoint, source, target, prior, later, top, bottom, conductivity,
    )
    got = lax.all_to_all(sent, "tm", 0, 0, tiled=True).reshape(blocks * span, LANES)
    line = half * depth
    own, up, down = call(
        functools.partial(forward_kernel, (blocks, span, planes, rows)),
        [f32(rows * line, LANES), f32(DEEP * line, LANES), f32(DEEP * line, LANES)],
        [pltpu.VMEM((span // 4 * planes * rows, 4 * LANES), jnp.float32)],
        6 * 10**8,
        4 * 10**6,
        got, forward_high, forward_low,
    )
    above = shift(down, "space", 1, False)
    below = shift(up, "space", -1, False)

    def unpack(packed):
        return packed[-slab_rows.shape[0]:].reshape(planes, rows, LANES)[..., :span]

    kappa = jnp.concatenate([unpack(top), slab, unpack(bottom)], axis=1)
    kappa = kappa.reshape(planes, 3 * rows, 2, half).transpose(1, 3, 2, 0).reshape(3 * rows, half, depth, 1)
    kappa = jnp.broadcast_to(kappa, (3 * rows, half, depth, LANES))
    tall = rows + 2 * DEEP
    tile = (half, depth, LANES)
    back = call(
        functools.partial(sweep_kernel, (blocks, half, planes, rows)),
        f32(blocks * own_cols, LANES),
        [pltpu.VMEM((tall, *tile), jnp.float32)] * 9
        + [pltpu.VMEM((own_cols // 4 * planes * rows, 4 * LANES), jnp.float32)],
        10**9,
        6 * 10**6,
        own.reshape(rows, *tile), above.reshape(DEEP, *tile), below.reshape(DEEP, *tile), kappa, shifts, inverse_high, inverse_low,
    )
    got_back = lax.all_to_all(back, "tm", 0, 0, tiled=True)
    return tuple(
        call(update_kernel, [f32(*state.shape), f32(*state.shape)], [], 10**6, 2 * 10**6, got_back, state, adjoint)
    )


def solution(mesh):
    split = P("tm", None, "space", None)
    return jax.shard_map(
        body,
        mesh=mesh,
        in_specs=(split, split, split, split, P(None, "space", None)),
        out_specs=(split, split),
        check_vma=False,
    )
```

time: 479 us -> 125 us (0.26)
  the two profiles are of different devices: /device:TPU:2 before, /device:TPU:41 now
where the time goes in v1:
time: 125 us
  blocking collectives  55.3 us (44%)
  Pallas kernels  30.8 us (25%)
  starting transfers between devices  16.3 us (13%)
  local copies, waits for them, and re-layouts  11 us (9%)
  waiting for transfers between devices  10.3 us (8%)
    all_to_all x1, blocking collectives, body(): lax.all_to_all(sent, 'tm', 0, 0, tiled=True).reshape(blocks * span, LANES)  33 us
    pallas_call x4, Pallas kernels, call(): pl.pallas_call(kernel, out_shape=outs, in_specs=[pl.BlockSpec(memory_spac...  30.8 us
    all_to_all x1, blocking collectives, body(): got_back = lax.all_to_all(back, 'tm', 0, 0, tiled=True)  22.3 us
    ppermute x6, starting transfers between devices, shift(): return lax.ppermute(block, axis, route)  16.3 us
    ppermute x6, waiting for transfers between devices, shift(): return lax.ppermute(block, axis, route)  10.3 us
    unnamed x18, local copies, waits for them, and re-layouts  2.88 us
  transfers between devices with their start and end apart: 6, of which 4 were waited for; matrix products, arithmetic and copies ran while one was open for 6% of the time, Pallas kernels for 0%

profile of v1, /device:TPU:41, one launch (start us, length us, event | category | flops | bytes accessed | tf_op | source)
XLA Modules:
  0.0 124.6 jit_solution(15013907011680339810)
XLA Ops:
  0.6 0.9 slice_bitcast_fusion
  1.5 0.1 collective-permute-start.1
  1.6 0.9 slice_bitcast_fusion.1
  2.6 1.7 %collective-permute-start = (f32[4,8,1024]{2,1,0:T(8,128)S(1)}, f32[4,8,1024]{2,1,0:T(8,128)S(1)}, u32[]{:S(2)}, u32[]{:S(2)}) collective-permute-start(f32[4,8,1024]{2,1,0:T(8,128)S(1)} %slice_bitcast_fusion.1), channel_id=1, source_target_pairs={{0,8},{8,16},{16,24},{24,32},{32,40},{40,48},{48,56},{56,64},{64,7... | collective-permute-start | bytes 393224 | tf_op jit(solution)/shard_map/ppermute | solution.py:255
  4.3 1.1 slice_bitcast_fusion.3
  5.4 1.1 slice_bitcast_fusion.2
  6.4 1.0 fusion
  7.5 0.9 pad_dynamic-slice_fusion
  8.4 0.1 pad_maximum_fusion.2
  8.7 3.0 %collective-permute-start.3 = (f32[24,1024]{1,0:T(8,128)S(1)}, f32[24,1024]{1,0:T(8,128)S(1)}, u32[]{:S(2)}, u32[]{:S(2)}) collective-permute-start(f32[24,1024]{1,0:T(8,128)S(1)} %get-tuple-element.14), channel_id=1, source_target_pairs={{1,0},{2,1},{3,2},{4,3},{5,4},{6,5},{7,6},{9,8},{10,9},{11,10},{12... | collective-permute-start | bytes 294920 | tf_op jit(solution)/shard_map/ppermute | solution.py:255
  11.6 3.1 %collective-permute-start.2 = (f32[24,1024]{1,0:T(8,128)S(1)}, f32[24,1024]{1,0:T(8,128)S(1)}, u32[]{:S(2)}, u32[]{:S(2)}) collective-permute-start(f32[24,1024]{1,0:T(8,128)S(1)} %get-tuple-element.15), channel_id=1, source_target_pairs={{0,1},{1,2},{2,3},{3,4},{4,5},{5,6},{6,7},{8,9},{9,10},{10,11},{11... | collective-permute-start | bytes 294920 | tf_op jit(solution)/shard_map/ppermute | solution.py:255
  14.7 0.4 collective-permute-done.3.bottom
  15.1 1.3 %collective-permute-done.2.top = f32[24,1024]{1,0:T(8,128)S(1)} collective-permute-done((f32[24,1024]{1,0:T(8,128)S(1)}, f32[24,1024]{1,0:T(8,128)S(1)}, u32[]{:S(2)}, u32[]{:S(2)}) %collective-permute-start.2) | collective-permute-done | bytes 98336 | tf_op jit(solution)/shard_map/ppermute | solution.py:255
  16.4 0.0 collective-permute-done.prior
  16.4 0.6 copy-done.3
  17.0 0.1 copy-done.4
  17.0 0.7 copy-done.5
  17.7 3.0 %shard_map.113 = f32[32,48,128]{2,1,0:T(8,128)} custom-call(f32[2,4,8,1024]{3,2,1,0:T(8,128)} %state.3, f32[2,4,8,1024]{3,2,1,0:T(8,128)} %adjoint.3, f32[2,4,8,1024]{3,2,1,0:T(8,128)} %source.1, f32[2,4,8,1024]{3,2,1,0:T(8,128)} %target.1, f32[4,8,1024]{2,1,0:T(8,128)} %copy-done.5, f32[4,8,1024]{2,1,0:T(8,128)} %copy-done.4, f32[24,1024]{1,0:T(8,128)} %copy-done.3, ...), custom_call_target="tpu_custom_call" | custom-call | flops 10000000 | bytes 3000000 | tf_op jit(solution)/shard_map/pallas_call | solution.py:237
  20.7 33.0 %all_to_all.16 = f32[32,48,128]{2,1,0:T(8,128)} all-to-all(f32[32,48,128]{2,1,0:T(8,128)} %shard_map.113), channel_id=1, replica_groups=mesh['tm'=32,'space'=8] {'tm'}, dimensions={0} | all-to-all | bytes 1572864 | tf_op jit(solution)/shard_map/all_to_all | solution.py:296
  53.8 4.3 %shard_map.114 = (f32[1536,128]{1,0:T(8,128)}, f32[1344,128]{1,0:T(8,128)}, f32[1344,128]{1,0:T(8,128)}) custom-call(f32[1536,128]{1,0:T(8,128)} %bitcast.44, bf16[512,512]{1,0:T(8,128)(2,1)} %constant.24.clone.high, bf16[512,512]{1,0:T(8,128)(2,1)} %constant.25.clone.low), custom_call_target="tpu_custom_call" | custom-call | flops 600000000 | bytes 4000000 | tf_op jit(solution)/shard_map/pallas_call | solution.py:237
  58.0 6.5 %collective-permute-start.4 = (f32[1344,128]{1,0:T(8,128)}, f32[1344,128]{1,0:T(8,128)S(1)}, u32[]{:S(2)}, u32[]{:S(2)}) collective-permute-start(f32[1344,128]{1,0:T(8,128)} %get-tuple-element.6), channel_id=1, source_target_pairs={{0,1},{1,2},{2,3},{3,4},{4,5},{5,6},{6,7},{8,9},{9,10},{10,11},{11... | collective-permute-start | bytes 2064392 | tf_op jit(solution)/shard_map/ppermute | solution.py:255
  64.6 1.9 %collective-permute-start.5 = (f32[1344,128]{1,0:T(8,128)}, f32[1344,128]{1,0:T(8,128)S(1)}, u32[]{:S(2)}, u32[]{:S(2)}) collective-permute-start(f32[1344,128]{1,0:T(8,128)} %get-tuple-element.7), channel_id=1, source_target_pairs={{1,0},{2,1},{3,2},{4,3},{5,4},{6,5},{7,6},{9,8},{10,9},{11,10},{12... | collective-permute-start | bytes 2064392 | tf_op jit(solution)/shard_map/ppermute | solution.py:255
  66.5 0.8 slice_bitcast_fusion.6
  67.3 0.8 slice_bitcast_fusion.7
  68.0 0.1 reshape.47
  68.2 0.1 copy.27
  68.3 4.4 %collective-permute-done.4 = f32[1344,128]{1,0:T(8,128)S(1)} collective-permute-done((f32[1344,128]{1,0:T(8,128)}, f32[1344,128]{1,0:T(8,128)S(1)}, u32[]{:S(2)}, u32[]{:S(2)}) %collective-permute-start.4) | collective-permute-done | bytes 688160 | tf_op jit(solution)/shard_map/ppermute | solution.py:255
  72.7 4.3 %collective-permute-done.5 = f32[1344,128]{1,0:T(8,128)S(1)} collective-permute-done((f32[1344,128]{1,0:T(8,128)}, f32[1344,128]{1,0:T(8,128)S(1)}, u32[]{:S(2)}, u32[]{:S(2)}) %collective-permute-start.5) | collective-permute-done | bytes 688160 | tf_op jit(solution)/shard_map/ppermute | solution.py:255
  77.0 1.8 %broadcast_in_dim.8.kappa = f32[24,24,8,128]{3,2,1,0:T(8,128)} broadcast(f32[24,24,8]{2,1,0:T(8,128)S(1)} %copy.27), dimensions={0,1,2} | broadcast | bytes 2377728 | tf_op jit(solution)/shard_map/broadcast_in_dim | solution.py:314
  78.8 21.3 %shard_map.115 = f32[1024,128]{1,0:T(8,128)} custom-call(f32[8,24,8,128]{3,2,1,0:T(8,128)} %bitcast.43, f32[7,24,8,128]{3,2,1,0:T(8,128)} %bitcast.45, f32[7,24,8,128]{3,2,1,0:T(8,128)} %bitcast.46, f32[24,24,8,128]{3,2,1,0:T(8,128)} %broadcast_in_dim.8.kappa, f32[2,128]{1,0:T(2,128)} %constant.26.clone.shifts, bf16[512,512]{1,0:T(8,128)(2,1)} %constant.27.clone.high, ...), custom_call_target="tpu_custom_call" | custom-call | flops 1000000000 | bytes 6000000 | tf_op jit(solution)/shard_map/pallas_call | solution.py:237
  100.1 22.3 %all_to_all.17 = f32[32,32,128]{2,1,0:T(8,128)} all-to-all(f32[32,32,128]{2,1,0:T(8,128)} %bitcast.41), channel_id=1, replica_groups=mesh['tm'=32,'space'=8] {'tm'}, dimensions={0} | all-to-all | bytes 1048576 | tf_op jit(solution)/shard_map/all_to_all | solution.py:326
  122.4 2.2 %shard_map.116 = (f32[2,4,8,1024]{3,2,1,0:T(8,128)}, f32[2,4,8,1024]{3,2,1,0:T(8,128)}) custom-call(f32[1024,128]{1,0:T(8,128)} %bitcast.42, f32[2,4,8,1024]{3,2,1,0:T(8,128)} %state.3, f32[2,4,8,1024]{3,2,1,0:T(8,128)} %adjoint.3), custom_call_target="tpu_custom_call" | custom-call | flops 1000000 | bytes 2000000 | tf_op jit(solution)/shard_map/pallas_call | solution.py:237
  (22 shorter events, 0.2 us)
Async XLA Ops:
  1.5 14.8 %collective-permute-start.1 = (f32[4,8,1024]{2,1,0:T(8,128)S(1)}, f32[4,8,1024]{2,1,0:T(8,128)S(1)}, u32[]{:S(2)}, u32[]{:S(2)}) collective-permute-start(f32[4,8,1024]{2,1,0:T(8,128)S(1)} %slice_bitcast_fusion), channel_id=1, source_target_pairs={{0,248},{8,0},{16,8},{24,16},{32,24},{40,32},{48,40},{56,48},{64,5... | collective-permute-start | bytes 393224 | tf_op jit(solution)/shard_map/ppermute | solution.py:255
  2.6 13.8 %collective-permute-start = (f32[4,8,1024]{2,1,0:T(8,128)S(1)}, f32[4,8,1024]{2,1,0:T(8,128)S(1)}, u32[]{:S(2)}, u32[]{:S(2)}) collective-permute-start(f32[4,8,1024]{2,1,0:T(8,128)S(1)} %slice_bitcast_fusion.1), channel_id=1, source_target_pairs={{0,8},{8,16},{16,24},{24,32},{32,40},{40,48},{48,56},{56,64},{64,7... | collective-permute-start | bytes 393224 | tf_op jit(solution)/shard_map/ppermute | solution.py:255
  8.7 6.4 %collective-permute-start.3 = (f32[24,1024]{1,0:T(8,128)S(1)}, f32[24,1024]{1,0:T(8,128)S(1)}, u32[]{:S(2)}, u32[]{:S(2)}) collective-permute-start(f32[24,1024]{1,0:T(8,128)S(1)} %get-tuple-element.14), channel_id=1, source_target_pairs={{1,0},{2,1},{3,2},{4,3},{5,4},{6,5},{7,6},{9,8},{10,9},{11,10},{12... | collective-permute-start | bytes 294920 | tf_op jit(solution)/shard_map/ppermute | solution.py:255
  11.6 4.7 %collective-permute-start.2 = (f32[24,1024]{1,0:T(8,128)S(1)}, f32[24,1024]{1,0:T(8,128)S(1)}, u32[]{:S(2)}, u32[]{:S(2)}) collective-permute-start(f32[24,1024]{1,0:T(8,128)S(1)} %get-tuple-element.15), channel_id=1, source_target_pairs={{0,1},{1,2},{2,3},{3,4},{4,5},{5,6},{6,7},{8,9},{9,10},{10,11},{11... | collective-permute-start | bytes 294920 | tf_op jit(solution)/shard_map/ppermute | solution.py:255
  15.1 1.3 %copy-start.2 = (f32[24,1024]{1,0:T(8,128)}, f32[24,1024]{1,0:T(8,128)S(1)}, u32[]{:S(2)}) copy-start(f32[24,1024]{1,0:T(8,128)S(1)} %collective-permute-done.3.bottom) | copy-start | bytes 294916
  16.4 0.6 copy-start.3
  16.4 0.7 copy-start.4
  17.0 0.7 copy-start.5
  58.0 14.7 %collective-permute-start.4 = (f32[1344,128]{1,0:T(8,128)}, f32[1344,128]{1,0:T(8,128)S(1)}, u32[]{:S(2)}, u32[]{:S(2)}) collective-permute-start(f32[1344,128]{1,0:T(8,128)} %get-tuple-element.6), channel_id=1, source_target_pairs={{0,1},{1,2},{2,3},{3,4},{4,5},{5,6},{6,7},{8,9},{9,10},{10,11},{11... | collective-permute-start | bytes 2064392 | tf_op jit(solution)/shard_map/ppermute | solution.py:255
  64.6 12.5 %collective-permute-start.5 = (f32[1344,128]{1,0:T(8,128)}, f32[1344,128]{1,0:T(8,128)S(1)}, u32[]{:S(2)}, u32[]{:S(2)}) collective-permute-start(f32[1344,128]{1,0:T(8,128)} %get-tuple-element.7), channel_id=1, source_target_pairs={{1,0},{2,1},{3,2},{4,3},{5,4},{6,5},{7,6},{9,8},{10,9},{11,10},{12... | collective-permute-start | bytes 2064392 | tf_op jit(solution)/shard_map/ppermute | solution.py:255
  72.7 6.1 %copy-start = (f32[1344,128]{1,0:T(8,128)}, f32[1344,128]{1,0:T(8,128)S(1)}, u32[]{:S(2)}) copy-start(f32[1344,128]{1,0:T(8,128)S(1)} %collective-permute-done.4) | copy-start | bytes 2064388
  77.0 1.8 %copy-start.1 = (f32[1344,128]{1,0:T(8,128)}, f32[1344,128]{1,0:T(8,128)S(1)}, u32[]{:S(2)}) copy-start(f32[1344,128]{1,0:T(8,128)S(1)} %collective-permute-done.5) | copy-start | bytes 2064388

commit v2 on v1

v2 whole, which is shorter than its diff:
```python
import functools
import math

import jax
import jax.numpy as jnp
import ml_dtypes
import numpy as np
from jax import lax
from jax.experimental import pallas as pl
from jax.experimental.pallas import tpu as pltpu
from jax.sharding import PartitionSpec as P

SWEEPS = 8
STEP = 0.5
PENALTY = 0.05
LANES = 128
WIDE = 8
DEEP = SWEEPS - 1
SUBLANES = 8
VMEM_LIMIT = 28 * 1024 * 1024


def transforms(period):
    q = STEP / PENALTY
    time = np.arange(period)
    pairs = [(0, 1)] + [(k, s) for k in range(1, period // 2) for s in (1, -1)] + [(period // 2, 1)]
    count = len(pairs)
    forward = np.zeros((period, 2, 2 * count))
    inverse = np.zeros((2 * count, period, 2))
    real_shift, imag_shift = np.zeros(count), np.zeros(count)
    for m, (k, sign) in enumerate(pairs):
        theta = 2.0 * math.pi * k / period
        sine = 0.0 if k in (0, period // 2) else math.sin(theta)
        root = math.sqrt(sine * sine + STEP * q)
        real_shift[m] = 1.0 - math.cos(theta)
        imag_shift[m] = sign * root
        wave = np.exp(-1j * theta * time)
        first = (root + sign * sine) / (2.0 * q * root) * wave
        second = -sign * 1j / (2.0 * root) * wave
        for f, row in enumerate((first, second)):
            forward[:, f, m] = row.real
            forward[:, f, count + m] = row.imag
        weight = 2.0 / period
        back = np.conj(wave) * weight
        for f, factor in enumerate((q, sign * 1j * (root - sign * sine))):
            inverse[m, :, f] = (factor * back).real
            inverse[count + m, :, f] = -(factor * back).imag
    real_lane = np.concatenate([real_shift, real_shift])
    imag_lane = np.concatenate([imag_shift, -imag_shift])
    return forward, inverse, np.stack([real_lane, imag_lane]).astype(np.float32)


def split_const(matrix):
    high = matrix.astype(np.float32).astype(ml_dtypes.bfloat16)
    low = (matrix - high.astype(np.float64)).astype(np.float32).astype(ml_dtypes.bfloat16)
    return high, low


def dot_split(left, high_ref, low_ref):
    high = left.astype(jnp.bfloat16)
    low = (left - high.astype(jnp.float32)).astype(jnp.bfloat16)
    dot = functools.partial(jnp.dot, preferred_element_type=jnp.float32)
    return dot(high, high_ref[...]) + (dot(low, high_ref[...]) + dot(high, low_ref[...]))


def pack_kernel(own_cols, me, state, adjoint, cond, to_down, to_up, last, first):
    steps, planes, rows, cols = state.shape
    tiles = cols // LANES
    per_tile = 2 * steps * planes
    for out, r in ((to_down, rows - 1), (to_up, 0)):
        for k in range(tiles):
            lanes = pl.ds(k * LANES, LANES)
            for f, field in enumerate((state, adjoint)):
                for t in range(steps):
                    for p in range(planes):
                        out[pl.ds(k * per_tile + (f * steps + t) * planes + p, 1), :] = field[t, p, pl.ds(r, 1), lanes]
            for p in range(planes):
                out[pl.ds(tiles * per_tile + k * planes + p, 1), :] = cond[p, pl.ds(r, 1), lanes]
    start = me[0] * own_cols - WIDE
    column = lax.broadcasted_iota(jnp.int32, (rows, LANES), 1) + start
    base = tiles * (per_tile + planes)
    for p in range(planes):
        turned = pltpu.roll(cond[p], lax.rem(cols - start, cols), axis=1)[:, :LANES]
        slab = jnp.where((column >= 0) & (column < cols), turned, 0.0)
        to_down[pl.ds(base + p * rows, rows), :] = slab
        to_up[pl.ds(base + p * rows, rows), :] = slab
    last[...] = state[steps - 1]
    first[...] = adjoint[0]


def edge_row(packed, tiles, base, stride, at):
    return jnp.concatenate([packed[pl.ds(base + k * stride + at, 1), :] for k in range(tiles)], axis=1)


def local_kernel(state, adjoint, source, target, cond, out):
    steps, planes, rows, cols = state.shape
    row = lax.broadcasted_iota(jnp.int32, (rows, cols), 0)
    col = lax.broadcasted_iota(jnp.int32, (rows, cols), 1)

    def near(value):
        return (
            pltpu.roll(value, 1, axis=0),
            pltpu.roll(value, rows - 1, axis=0),
            jnp.where(col == 0, 0.0, pltpu.roll(value, 1, axis=1)),
            jnp.where(col == cols - 1, 0.0, pltpu.roll(value, cols - 1, axis=1)),
        )

    kappa = [cond[p] for p in range(planes)]
    zero = jnp.zeros((rows, cols), jnp.float32)
    for p in range(planes):
        around = near(kappa[p])
        around += (kappa[p - 1] if p else zero, kappa[p + 1] if p < planes - 1 else zero)
        weights = [(0.5 * STEP) * (kappa[p] + k) for k in around]
        weights[0] = jnp.where(row == 0, 0.0, weights[0])
        weights[1] = jnp.where(row == rows - 1, 0.0, weights[1])
        diag = weights[0]
        for w in weights[1:]:
            diag = diag + w
        for t in range(steps):
            stiff = []
            for field in (state, adjoint):
                value = field[t, p]
                total = diag * value
                for w, v in zip(weights, near(value)):
                    total = total - w * v
                if p:
                    total = total - weights[4] * field[t, p - 1]
                if p < planes - 1:
                    total = total - weights[5] * field[t, p + 1]
                stiff.append(total)
            s, a = state[t, p], adjoint[t, p]
            s_step = s - state[t - 1, p] if t else s
            a_step = a - adjoint[t + 1, p] if t < steps - 1 else a
            first = STEP * source[t, p] - (s_step + stiff[0] + (STEP / PENALTY) * a)
            second = -STEP * target[t, p] - (a_step + stiff[1] - STEP * s)
            for f, value in enumerate((first, second)):
                out[pl.ds(((t * 2 + f) * planes + p) * rows, rows), :] = value


def finish_kernel(blocks, partial, state, adjoint, prior, later, top, bottom, cond, out, res, turned):
    steps, planes, rows, cols = state.shape
    tiles = cols // LANES
    per_tile = 2 * steps * planes
    row = lax.broadcasted_iota(jnp.int32, (rows, cols), 0)
    for p in range(planes):
        weights = []
        for packed, r in ((top, 0), (bottom, rows - 1)):
            beyond = edge_row(packed, tiles, tiles * per_tile, planes, p)
            weights.append(jnp.where(row == r, (0.5 * STEP) * (cond[p] + beyond), 0.0))
        for t in range(steps):
            for f, field in enumerate((state, adjoint)):
                at = ((t * 2 + f) * planes + p) * rows
                edge = (f * steps + t) * planes + p
                value = field[t, p]
                total = partial[pl.ds(at, rows), :]
                for packed, w in zip((top, bottom), weights):
                    total = total - w * (value - edge_row(packed, tiles, 0, per_tile, edge))
                if f == 0 and t == 0:
                    total = total + prior[p]
                if f == 1 and t == steps - 1:
                    total = total + later[p]
                res[pl.ds(at, rows), :] = total
    turned[pl.ds(0, WIDE), :] = jnp.zeros((WIDE, LANES), jnp.float32)
    turned[pl.ds(WIDE + cols, WIDE), :] = jnp.zeros((WIDE, LANES), jnp.float32)
    for tile in range(tiles):
        turned[pl.ds(WIDE + tile * LANES, LANES), :] = res[:, pl.ds(tile * LANES, LANES)].T
    own = cols // blocks
    for j in range(blocks):
        out[j] = turned[pl.ds(j * own, own + 2 * WIDE), :]


def column_group(g, span):
    near = [2 * g, 2 * g + 1]
    return near + [span - 1 - c for c in near]


def forward_kernel(shape, got, high, low, own, up, down, left):
    blocks, span, planes, rows = shape
    strip = span // (2 * SUBLANES)
    line = planes * span
    cells = planes * rows
    for g in range(span // 4):
        parts = [got[pl.ds(c, blocks, stride=span), :] for c in column_group(g, span)]
        turned = jnp.concatenate(parts, axis=0).T
        for tf in range(4):
            left[pl.ds(g * cells, cells), pl.ds(tf * LANES, LANES)] = turned[tf * cells : (tf + 1) * cells]
    spectrum = dot_split(left[...], high, low)
    for g in range(span // 4):
        for pair in range(2):
            sub, at = divmod(2 * g + pair, strip)
            for part in range(2):
                lane = (2 * pair + part) * LANES
                for p in range(planes):
                    piece = spectrum[g * cells + p * rows : g * cells + (p + 1) * rows, lane : lane + LANES]
                    begin = ((p * strip + at) * 2 + part) * SUBLANES + sub
                    own[pl.ds(begin, rows, stride=line), :] = piece
    up[...] = own[pl.ds(0, line * DEEP), :]
    down[...] = own[pl.ds(line, line * DEEP), :]


def weight_kernel(shape, kappa, shifts, w_row, w_col, w_plane, scale, cross, wide):
    planes, strip = shape
    count = planes * strip
    tall = scale.shape[0]
    sub = lax.broadcasted_iota(jnp.int32, (SUBLANES, LANES), 0)
    mirrored = lax.broadcasted_iota(jnp.int32, (SUBLANES, LANES), 1) >= LANES // 2
    real = jnp.broadcast_to(shifts[0:1, :], (SUBLANES, LANES))
    imag = jnp.broadcast_to(shifts[1:2, :], (SUBLANES, LANES))

    def spread(r, _):
        packed = kappa[r]
        for n in range(count):
            a = jnp.broadcast_to(packed[:, n : n + 1], (SUBLANES, LANES))
            b = jnp.broadcast_to(packed[:, count + n : count + n + 1], (SUBLANES, LANES))
            wide[r, n] = jnp.where(mirrored, b, a)

    def bond(a, b):
        return jnp.where(a * b > 0.0, (0.5 * STEP) * (a + b), 0.0)

    def setup(r, _):
        here = [wide[r + 1, n] for n in range(count)]
        for p in range(planes):
            for c in range(strip):
                n = p * strip + c
                mine = here[n]
                if c:
                    to_left = here[n - 1]
                else:
                    to_left = jnp.where(sub == 0, 0.0, pltpu.roll(here[n + strip - 1], 1, axis=0))
                    w_col[r, p * (strip + 1)] = bond(mine, to_left)
                if c < strip - 1:
                    to_right = here[n + 1]
                else:
                    to_right = pltpu.roll(here[n - strip + 1], SUBLANES - 1, axis=0)
                    to_right = jnp.where(sub == SUBLANES - 1, pltpu.roll(mine, LANES // 2, axis=1), to_right)
                w_col[r, p * (strip + 1) + c + 1] = bond(mine, to_right)
                below = wide[r + 2, n]
                w_row[r, n] = bond(mine, below)
                around = wide[r, n] + below + to_left + to_right
                if p:
                    around = around + here[n - strip]
                if p < planes - 1:
                    around = around + here[n + strip]
                    w_plane[r, n] = bond(mine, here[n + strip])
                big = (0.5 * STEP) * (6.0 * mine + around) + real
                inv = 1.0 / (big * big + imag * imag)
                scale[r, n] = big * inv
                cross[r, n] = imag * inv

    lax.fori_loop(0, tall + 2, spread, None)
    lax.fori_loop(0, tall, setup, None)


def sweep_kernel(shape, own, above, below, w_row, w_col, w_plane, scale, cross, high, low, out, rhs, first, second, left):
    blocks, own_cols, planes, strip = shape
    rows = own.shape[0]
    tall = rows + 2 * DEEP
    count = planes * strip
    line = 2 * count * SUBLANES
    sub = lax.broadcasted_iota(jnp.int32, (SUBLANES, LANES), 0)

    def at(r, n):
        return pl.ds(pl.multiple_of((r * 2 * count + n) * SUBLANES, SUBLANES), SUBLANES)

    def solve(target, totals, r, m):
        a, b = scale[r, m], cross[r, m]
        target[at(r, 2 * m), :] = a * totals[0] + b * totals[1]
        target[at(r, 2 * m + 1), :] = a * totals[1] - b * totals[0]

    for source, offset in ((above, 0), (own, DEEP), (below, DEEP + rows)):

        def start(r, _, source=source, offset=offset):
            for m in range(count):
                pair = [source[r, 2 * m + k] for k in range(2)]
                for k in range(2):
                    rhs[r + offset, 2 * m + k] = pair[k]
                solve(first, pair, r + offset, m)

        lax.fori_loop(0, source.shape[0], start, None)

    def relax(old, new, r):
        here = [[old[at(r, 2 * m + k), :] for k in range(2)] for m in range(count)]
        for p in range(planes):
            base = p * strip
            before = [pltpu.roll(v, 1, axis=0) for v in here[base + strip - 1]]
            across = [pltpu.roll(v, LANES // 2, axis=1) for v in here[base + strip - 1]]
            after = [pltpu.roll(v, SUBLANES - 1, axis=0) for v in here[base]]
            after = [jnp.where(sub == SUBLANES - 1, x, v) for x, v in zip(across, after)]
            for c in range(strip):
                m = base + c
                flank = p * (strip + 1) + c
                totals = []
                for k in range(2):
                    to_left = here[m - 1][k] if c else before[k]
                    to_right = here[m + 1][k] if c < strip - 1 else after[k]
                    total = w_col[r, flank] * to_left + w_col[r, flank + 1] * to_right
                    others = w_row[r, m] * old[at(r + 1, 2 * m + k), :] + w_row[r - 1, m] * old[at(r - 1, 2 * m + k), :]
                    mine = rhs[r, 2 * m + k]
                    if p:
                        mine = mine + w_plane[r, m - strip] * here[m - strip][k]
                    if p < planes - 1:
                        others = others + w_plane[r, m] * here[m + strip][k]
                    totals.append(mine + (total + others))
                solve(new, totals, r, m)

    old, new = first, second
    for sweep in range(1, SWEEPS):

        def step(q, _, old=old, new=new, sweep=sweep):
            relax(old, new, sweep + 2 * q)
            relax(old, new, sweep + 2 * q + 1)

        lax.fori_loop(0, (tall - 2 * sweep) // 2, step, None)
        old, new = new, old

    cells = planes * rows
    for g in range(own_cols // 4):
        for pair in range(2):
            side, place = divmod(2 * g + pair + WIDE, strip)
            for part in range(2):
                for p in range(planes):
                    begin = DEEP * line + ((p * strip + place) * 2 + part) * SUBLANES + side
                    piece = old[pl.ds(begin, rows, stride=line), :]
                    left[pl.ds(g * cells + p * rows, rows), pl.ds((2 * pair + part) * LANES, LANES)] = piece
    values = dot_split(left[...], high, low)
    for g in range(own_cols // 4):
        parts = [values[g * cells : (g + 1) * cells, tf * LANES : (tf + 1) * LANES] for tf in range(4)]
        turned = jnp.concatenate(parts, axis=0).T
        for c, column in enumerate(column_group(g, own_cols)):
            out[pl.ds(column, blocks, stride=own_cols), :] = turned[c * blocks : (c + 1) * blocks]


def update_kernel(got, state, adjoint, new_state, new_adjoint):
    steps, planes, rows, cols = state.shape
    for tile in range(cols // LANES):
        block = got[pl.ds(tile * LANES, LANES), :].T
        for t in range(steps):
            for f, (old, new) in enumerate(((state, new_state), (adjoint, new_adjoint))):
                for p in range(planes):
                    at = ((t * 2 + f) * planes + p) * rows
                    new[t, p, :, pl.ds(tile * LANES, LANES)] = (
                        old[t, p, :, pl.ds(tile * LANES, LANES)] + block[at : at + rows]
                    )


def call(kernel, outs, scratch, flops, moved, *args, scalars=0):
    vmem = pl.BlockSpec(memory_space=pltpu.VMEM)
    smem = pl.BlockSpec(memory_space=pltpu.SMEM)
    return pl.pallas_call(
        kernel,
        out_shape=outs,
        in_specs=[smem] * scalars + [vmem] * (len(args) - scalars),
        out_specs=[vmem] * len(outs) if isinstance(outs, list) else vmem,
        scratch_shapes=scratch,
        compiler_params=pltpu.CompilerParams(vmem_limit_bytes=VMEM_LIMIT),
        cost_estimate=pl.CostEstimate(flops=flops, bytes_accessed=moved, transcendentals=0),
    )(*args)


def f32(*shape):
    return jax.ShapeDtypeStruct(shape, jnp.float32)


def shift(block, axis, distance, wrap):
    count = lax.axis_size(axis)
    route = [(i, (i + distance) % count) for i in range(count) if wrap or 0 <= i + distance < count]
    return lax.ppermute(block, axis, route)


def body(state, adjoint, source, target, conductivity):
    steps, planes, rows, cols = state.shape
    blocks = lax.axis_size("tm")
    me = lax.axis_index("tm")
    own_cols = cols // blocks
    span = own_cols + 2 * WIDE
    strip = span // (2 * SUBLANES)
    count = planes * strip
    line = 2 * count * SUBLANES
    tall = rows + 2 * DEEP
    tiles = cols // LANES
    tile = (SUBLANES, LANES)

    forward, inverse, shifts = transforms(steps * blocks)
    same = np.eye(4).reshape(4, 2, 2)
    forward = forward.reshape(blocks, steps * 2, 2, LANES // 2)
    forward = np.einsum("itks,chp->tcipkhs", forward, same).reshape(4 * LANES, 4 * LANES)
    inverse = inverse.reshape(2, LANES // 2, blocks, steps * 2)
    inverse = np.einsum("ksit,chp->pkhstci", inverse, same).reshape(4 * LANES, 4 * LANES)
    forward_high, forward_low = split_const(forward)
    inverse_high, inverse_low = split_const(inverse)

    edges = tiles * planes * (2 * steps + 1) + planes * rows
    to_down, to_up, last, first = call(
        functools.partial(pack_kernel, own_cols),
        [f32(edges, LANES), f32(edges, LANES), f32(planes, rows, cols), f32(planes, rows, cols)],
        [],
        10**5,
        10**6,
        me.reshape(1), state, adjoint, conductivity,
        scalars=1,
    )
    top = shift(to_down, "space", 1, False)
    bottom = shift(to_up, "space", -1, False)
    prior = shift(last, "tm", 1, True)
    later = shift(first, "tm", -1, True)
    partial = call(
        local_kernel,
        f32(LANES, cols),
        [],
        10**7,
        3 * 10**6,
        state, adjoint, source, target, conductivity,
    )
    sent = call(
        functools.partial(finish_kernel, blocks),
        f32(blocks, span, LANES),
        [pltpu.VMEM((LANES, cols), jnp.float32), pltpu.VMEM((cols + 2 * WIDE, LANES), jnp.float32)],
        10**7,
        3 * 10**6,
        partial, state, adjoint, prior, later, top, bottom, conductivity,
    )
    got = lax.all_to_all(sent, "tm", 0, 0, tiled=True).reshape(blocks * span, LANES)
    own, up, down = call(
        functools.partial(forward_kernel, (blocks, span, planes, rows)),
        [f32(rows * line, LANES), f32(DEEP * line, LANES), f32(DEEP * line, LANES)],
        [pltpu.VMEM((span // 4 * planes * rows, 4 * LANES), jnp.float32)],
        6 * 10**8,
        4 * 10**6,
        got, forward_high, forward_low,
    )
    above = shift(down, "space", 1, False)
    below = shift(up, "space", -1, False)

    def unpack(packed):
        return packed[edges - planes * rows :].reshape(planes, rows, LANES)[..., :span]

    kappa = jnp.concatenate([unpack(top), unpack(to_up), unpack(bottom)], axis=1)
    kappa = jnp.stack([kappa[..., : span // 2], kappa[..., : span // 2 - 1 : -1]], axis=2)
    kappa = kappa.reshape(planes, 3 * rows, 2, SUBLANES, strip).transpose(1, 3, 2, 0, 4).reshape(3 * rows, SUBLANES, 2 * count)
    kappa = jnp.pad(kappa, ((0, 0), (0, 0), (0, LANES - 2 * count)))
    weights = call(
        functools.partial(weight_kernel, (planes, strip)),
        [
            f32(tall, count, *tile),
            f32(tall, planes * (strip + 1), *tile),
            f32(tall, count - strip, *tile),
            f32(tall, count, *tile),
            f32(tall, count, *tile),
        ],
        [pltpu.VMEM((3 * rows, count, *tile), jnp.float32)],
        10**9,
        10**7,
        kappa, np.tile(shifts.reshape(2, 2, -1)[:, :1], (1, 2, 1)).reshape(2, LANES),
    )
    back = call(
        functools.partial(sweep_kernel, (blocks, own_cols, planes, strip)),
        f32(blocks * own_cols, LANES),
        [
            pltpu.VMEM((tall, 2 * count, *tile), jnp.float32),
            pltpu.VMEM((tall * line, LANES), jnp.float32),
            pltpu.VMEM((tall * line, LANES), jnp.float32),
            pltpu.VMEM((own_cols // 4 * planes * rows, 4 * LANES), jnp.float32),
        ],
        10**9,
        6 * 10**6,
        own.reshape(rows, 2 * count, *tile), above.reshape(DEEP, 2 * count, *tile), below.reshape(DEEP, 2 * count, *tile),
        *weights, inverse_high, inverse_low,
    )
    got_back = lax.all_to_all(back, "tm", 0, 0, tiled=True)
    return tuple(
        call(update_kernel, [f32(*state.shape), f32(*state.shape)], [], 10**6, 2 * 10**6, got_back, state, adjoint)
    )


def solution(mesh):
    split = P("tm", None, "space", None)
    return jax.shard_map(
        body,
        mesh=mesh,
        in_specs=(split, split, split, split, P(None, "space", None)),
        out_specs=(split, split),
        check_vma=False,
    )
```

time: 125 us -> 103 us (0.82)
  blocking collectives: 55.3 us -> 22.2 us
  waiting for transfers between devices: 10.3 us -> 28.2 us
  Pallas kernels: 30.8 us -> 17.2 us
  starting transfers between devices: 16.3 us -> 26.3 us
  local copies, waits for them, and re-layouts: 11 us -> 7.11 us
    all_to_all x1 -> x0, blocking collectives: 33 us -> none  [body(): lax.all_to_all(sent, 'tm', 0, 0, tiled=True).reshape(blocks * span, LANES)]
    all_to_all x0 -> x1, waiting for transfers between devices: none -> 22.3 us  [body(): lax.all_to_all(sent, 'tm', 0, 0, tiled=True).reshape(blocks * span, LANES)]
    pallas_call x4 -> x7, Pallas kernels: 30.8 us -> 17.2 us  [call(): pl.pallas_call(kernel, out_shape=outs, in_specs=[smem] * scalars + [vmem]...]
    all_to_all x0 -> x1, starting transfers between devices: none -> 12 us  [body(): lax.all_to_all(sent, 'tm', 0, 0, tiled=True).reshape(blocks * span, LANES)]
    ppermute x6, waiting for transfers between devices: 10.3 us -> 5.87 us  [shift(): return lax.ppermute(block, axis, route)]
    unnamed x18 -> x29, local copies, waits for them, and re-layouts: 2.88 us -> 6.96 us
    another operation x4 -> x0, local copies, waits for them, and re-layouts: 2.21 us -> none  [edge(): jnp.stack([state[:, :, r], adjoint[:, :, r]])]
    ppermute x6, starting transfers between devices: 16.3 us -> 14.3 us  [shift(): return lax.ppermute(block, axis, route)]
  transfers between devices with their start and end apart: 6 -> 7, of which waited for: 4 -> 4; matrix products, arithmetic and copies ran while one was open for 6% -> 1% of each run, Pallas kernels for 0% -> 5%
where the time goes in v2:
time: 103 us; the launch traced here: 102 us
  waiting for transfers between devices  28.2 us (27%)
  starting transfers between devices  26.3 us (26%)
  blocking collectives  22.2 us (22%)
  Pallas kernels  17.2 us (17%)
  local copies, waits for them, and re-layouts  7.11 us (7%)
    all_to_all x1, waiting for transfers between devices, body(): lax.all_to_all(sent, 'tm', 0, 0, tiled=True).reshape(blocks * span, LANES)  22.3 us
    all_to_all x1, blocking collectives, body(): got_back = lax.all_to_all(back, 'tm', 0, 0, tiled=True)  22.2 us
    pallas_call x7, Pallas kernels, call(): pl.pallas_call(kernel, out_shape=outs, in_specs=[smem] * scalars + [vmem]...  17.2 us
    ppermute x6, starting transfers between devices, shift(): return lax.ppermute(block, axis, route)  14.3 us
    all_to_all x1, starting transfers between devices, body(): lax.all_to_all(sent, 'tm', 0, 0, tiled=True).reshape(blocks * span, LANES)  12 us
    unnamed x29, local copies, waits for them, and re-layouts  6.96 us
    ppermute x6, waiting for transfers between devices, shift(): return lax.ppermute(block, axis, route)  5.87 us
  transfers between devices with their start and end apart: 7, of which 4 were waited for; matrix products, arithmetic and copies ran while one was open for 1% of the time, Pallas kernels for 5%

profile of v2, /device:TPU:41, one launch (start us, length us, event | category | flops | bytes accessed | tf_op | source)
XLA Modules:
  0.0 102.0 jit_solution(4527973868894983952)
XLA Ops:
  0.6 0.9 copy-done
  1.6 0.9 copy-done.2
  2.5 0.9 copy-done.4
  3.4 0.2 shard_map.114
  3.6 1.7 %collective-permute-start = (f32[4,8,1024]{2,1,0:T(8,128)S(1)}, f32[4,8,1024]{2,1,0:T(8,128)S(1)}, u32[]{:S(2)}, u32[]{:S(2)}) collective-permute-start(f32[4,8,1024]{2,1,0:T(8,128)S(1)} %get-tuple-element.14), channel_id=1, source_target_pairs={{0,8},{8,16},{16,24},{24,32},{32,40},{40,48},{48,56},{56,64},{64,7... | collective-permute-start | bytes 393224 | tf_op jit(solution)/shard_map/ppermute | solution.py:367
  5.3 4.1 %collective-permute-start.2 = (f32[192,128]{1,0:T(8,128)S(1)}, f32[192,128]{1,0:T(8,128)S(1)}, u32[]{:S(2)}, u32[]{:S(2)}) collective-permute-start(f32[192,128]{1,0:T(8,128)S(1)} %get-tuple-element.16), channel_id=1, source_target_pairs={{0,1},{1,2},{2,3},{3,4},{4,5},{5,6},{6,7},{8,9},{9,10},{10,11},{11... | collective-permute-start | bytes 294920 | tf_op jit(solution)/shard_map/ppermute | solution.py:367
  9.5 1.9 %collective-permute-start.3 = (f32[192,128]{1,0:T(8,128)S(1)}, f32[192,128]{1,0:T(8,128)S(1)}, u32[]{:S(2)}, u32[]{:S(2)}) collective-permute-start(f32[192,128]{1,0:T(8,128)S(1)} %get-tuple-element.17), channel_id=1, source_target_pairs={{1,0},{2,1},{3,2},{4,3},{5,4},{6,5},{7,6},{9,8},{10,9},{11,10},{12... | collective-permute-start | bytes 294920 | tf_op jit(solution)/shard_map/ppermute | solution.py:367
  11.4 0.9 copy-done.5
  12.3 0.9 copy-done.8
  13.2 0.9 copy-done.9
  14.2 0.6 shard_map.113.partial
  14.8 0.6 collective-permute-done.3.bottom
  15.4 1.1 %shard_map.115 = f32[32,48,128]{2,1,0:T(8,128)} custom-call(f32[128,1024]{1,0:T(8,128)S(1)} %shard_map.113.partial, f32[2,4,8,1024]{3,2,1,0:T(8,128)S(1)} %copy-done, f32[2,4,8,1024]{3,2,1,0:T(8,128)S(1)} %copy-done.2, f32[4,8,1024]{2,1,0:T(8,128)S(1)} %collective-permute-done.prior, f32[4,8,1024]{2,1,0:T(8,128)S(1)} %collective-permute-done.1.later, ...), custom_call_target="tpu_custom_call" | custom-call | flops 10000000 | bytes 3000000 | tf_op jit(solution)/shard_map/pallas_call | solution.py:349
  16.5 12.0 %all-to-all-start = ((f32[32,48,128]{2,1,0:T(8,128)}), f32[32,48,128]{2,1,0:T(8,128)S(1)}, u32[]{:S(2)}, u32[]{:S(2)}) async-start(f32[32,48,128]{2,1,0:T(8,128)} %shard_map.115), calls=%async_computation | async-start | bytes 1572864 | tf_op jit(solution)/shard_map/all_to_all | solution.py:422
  28.5 0.1 copy.18
  28.6 0.1 copy.17
  28.7 22.3 %all-to-all-done = f32[32,48,128]{2,1,0:T(8,128)S(1)} async-done(((f32[32,48,128]{2,1,0:T(8,128)}), f32[32,48,128]{2,1,0:T(8,128)S(1)}, u32[]{:S(2)}, u32[]{:S(2)}) %all-to-all-start) | async-done | bytes 786464 | tf_op jit(solution)/shard_map/all_to_all | solution.py:422
  51.0 1.0 %copy-done.11 = bf16[512,512]{1,0:T(8,128)(2,1)S(1)} copy-done((bf16[512,512]{1,0:T(8,128)(2,1)S(1)}, bf16[512,512]{1,0:T(8,128)(2,1)}, u32[]{:S(2)}) %copy-start.11) | copy-done | bytes 524312
  52.1 2.4 %shard_map.116 = (f32[1536,128]{1,0:T(8,128)S(1)}, f32[1344,128]{1,0:T(8,128)S(1)}, f32[1344,128]{1,0:T(8,128)}) custom-call(f32[1536,128]{1,0:T(8,128)S(1)} %bitcast.23, bf16[512,512]{1,0:T(8,128)(2,1)S(1)} %copy-done.11, bf16[512,512]{1,0:T(8,128)(2,1)S(1)} %copy-done.10), custom_call_target="tpu_custom_call" | custom-call | flops 600000000 | bytes 4000000 | tf_op jit(solution)/shard_map/pallas_call | solution.py:349
  54.4 4.6 %collective-permute-start.4 = (f32[1344,128]{1,0:T(8,128)}, f32[1344,128]{1,0:T(8,128)S(1)}, u32[]{:S(2)}, u32[]{:S(2)}) collective-permute-start(f32[1344,128]{1,0:T(8,128)} %get-tuple-element.19), channel_id=1, source_target_pairs={{0,1},{1,2},{2,3},{3,4},{4,5},{5,6},{6,7},{8,9},{9,10},{10,11},{11... | collective-permute-start | bytes 2064392 | tf_op jit(solution)/shard_map/ppermute | solution.py:367
  59.0 1.9 %collective-permute-start.5 = (f32[1344,128]{1,0:T(8,128)S(1)}, f32[1344,128]{1,0:T(8,128)S(1)}, u32[]{:S(2)}, u32[]{:S(2)}) collective-permute-start(f32[1344,128]{1,0:T(8,128)S(1)} %get-tuple-element.20), channel_id=1, source_target_pairs={{1,0},{2,1},{3,2},{4,3},{5,4},{6,5},{7,6},{9,8},{10,9},{11,10},{12... | collective-permute-start | bytes 2064392 | tf_op jit(solution)/shard_map/ppermute | solution.py:367
  61.0 0.1 copy.19
  61.1 0.2 pad_maximum_fusion
  61.3 0.1 copy.16
  61.5 0.0 copy-start.6
  61.5 0.0 copy-start.7
  61.5 4.5 %shard_map.117 = (f32[22,12,8,128]{3,2,1,0:T(8,128)S(1)}, f32[22,16,8,128]{3,2,1,0:T(8,128)S(1)}, f32[22,9,8,128]{3,2,1,0:T(8,128)S(1)}, f32[22,12,8,128]{3,2,1,0:T(8,128)S(1)}, f32[22,12,8,128]{3,2,1,0:T(8,128)S(1)}) custom-call(f32[24,8,128]{2,1,0:T(8,128)S(1)} %pad.4.kappa, f32[2,128]{1,0:T(2,128)S(1)} %copy-done.12), custom_call_target="tpu_custom_call" | custom-call | flops 1000000000 | bytes 10000000 | tf_op jit(solution)/shard_map/pallas_call | solution.py:349
  66.0 1.2 %collective-permute-done.4 = f32[1344,128]{1,0:T(8,128)S(1)} collective-permute-done((f32[1344,128]{1,0:T(8,128)}, f32[1344,128]{1,0:T(8,128)S(1)}, u32[]{:S(2)}, u32[]{:S(2)}) %collective-permute-start.4) | collective-permute-done | bytes 688160 | tf_op jit(solution)/shard_map/ppermute | solution.py:367
  67.2 4.1 %collective-permute-done.5 = f32[1344,128]{1,0:T(8,128)S(1)} collective-permute-done((f32[1344,128]{1,0:T(8,128)S(1)}, f32[1344,128]{1,0:T(8,128)S(1)}, u32[]{:S(2)}, u32[]{:S(2)}) %collective-permute-start.5) | collective-permute-done | bytes 688160 | tf_op jit(solution)/shard_map/ppermute | solution.py:367
  71.3 7.5 %shard_map.118 = f32[1024,128]{1,0:T(8,128)S(1)} custom-call(f32[8,24,8,128]{3,2,1,0:T(8,128)S(1)} %bitcast.24, f32[7,24,8,128]{3,2,1,0:T(8,128)S(1)} %bitcast.25, f32[7,24,8,128]{3,2,1,0:T(8,128)S(1)} %bitcast.26, f32[22,12,8,128]{3,2,1,0:T(8,128)S(1)} %get-tuple-element.21.w_row, f32[22,16,8,128]{3,2,1,0:T(8,128)S(1)} %get-tuple-element.22.w_col, ...), custom_call_target="tpu_custom_call" | custom-call | flops 1000000000 | bytes 6000000 | tf_op jit(solution)/shard_map/pallas_call | solution.py:349
  78.9 22.2 %all_to_all.16 = f32[32,32,128]{2,1,0:T(8,128)S(1)} all-to-all(f32[32,32,128]{2,1,0:T(8,128)S(1)} %bitcast.22), channel_id=1, replica_groups=mesh['tm'=32,'space'=8] {'tm'}, dimensions={0} | all-to-all | bytes 1048576 | tf_op jit(solution)/shard_map/all_to_all | solution.py:469
  101.0 1.0 shard_map.119
  (29 shorter events, 0.1 us)
Async XLA Ops:
  0.6 1.0 copy-start
  1.6 0.9 copy-start.2
  2.5 0.9 copy-start.4
  3.6 11.8 %collective-permute-start = (f32[4,8,1024]{2,1,0:T(8,128)S(1)}, f32[4,8,1024]{2,1,0:T(8,128)S(1)}, u32[]{:S(2)}, u32[]{:S(2)}) collective-permute-start(f32[4,8,1024]{2,1,0:T(8,128)S(1)} %get-tuple-element.14), channel_id=1, source_target_pairs={{0,8},{8,16},{16,24},{24,32},{32,40},{40,48},{48,56},{56,64},{64,7... | collective-permute-start | bytes 393224 | tf_op jit(solution)/shard_map/ppermute | solution.py:367
  5.3 10.1 %collective-permute-start.1 = (f32[4,8,1024]{2,1,0:T(8,128)S(1)}, f32[4,8,1024]{2,1,0:T(8,128)S(1)}, u32[]{:S(2)}, u32[]{:S(2)}) collective-permute-start(f32[4,8,1024]{2,1,0:T(8,128)S(1)} %get-tuple-element.15), channel_id=1, source_target_pairs={{0,248},{8,0},{16,8},{24,16},{32,24},{40,32},{48,40},{56,48},{64,5... | collective-permute-start | bytes 393224 | tf_op jit(solution)/shard_map/ppermute | solution.py:367
  5.3 9.5 %collective-permute-start.2 = (f32[192,128]{1,0:T(8,128)S(1)}, f32[192,128]{1,0:T(8,128)S(1)}, u32[]{:S(2)}, u32[]{:S(2)}) collective-permute-start(f32[192,128]{1,0:T(8,128)S(1)} %get-tuple-element.16), channel_id=1, source_target_pairs={{0,1},{1,2},{2,3},{3,4},{4,5},{5,6},{6,7},{8,9},{9,10},{10,11},{11... | collective-permute-start | bytes 294920 | tf_op jit(solution)/shard_map/ppermute | solution.py:367
  9.5 5.9 %collective-permute-start.3 = (f32[192,128]{1,0:T(8,128)S(1)}, f32[192,128]{1,0:T(8,128)S(1)}, u32[]{:S(2)}, u32[]{:S(2)}) collective-permute-start(f32[192,128]{1,0:T(8,128)S(1)} %get-tuple-element.17), channel_id=1, source_target_pairs={{1,0},{2,1},{3,2},{4,3},{5,4},{6,5},{7,6},{9,8},{10,9},{11,10},{12... | collective-permute-start | bytes 294920 | tf_op jit(solution)/shard_map/ppermute | solution.py:367
  11.4 0.9 copy-start.5
  12.3 0.9 copy-start.8
  13.2 0.9 copy-start.9
  16.5 34.5 %copy-start.10 = (bf16[512,512]{1,0:T(8,128)(2,1)S(1)}, bf16[512,512]{1,0:T(8,128)(2,1)}, u32[]{:S(2)}) copy-start(bf16[512,512]{1,0:T(8,128)(2,1)} %constant.20.clone.low) | copy-start | bytes 1572868
  16.5 34.5 %all-to-all-start = ((f32[32,48,128]{2,1,0:T(8,128)}), f32[32,48,128]{2,1,0:T(8,128)S(1)}, u32[]{:S(2)}, u32[]{:S(2)}) async-start(f32[32,48,128]{2,1,0:T(8,128)} %shard_map.115), calls=%async_computation | async-start | bytes 1572864 | tf_op jit(solution)/shard_map/all_to_all | solution.py:422
  51.0 1.0 %copy-start.11 = (bf16[512,512]{1,0:T(8,128)(2,1)S(1)}, bf16[512,512]{1,0:T(8,128)(2,1)}, u32[]{:S(2)}) copy-start(bf16[512,512]{1,0:T(8,128)(2,1)} %constant.19.clone.high) | copy-start | bytes 1572868
  54.4 7.1 %copy-start.12 = (f32[2,128]{1,0:T(2,128)S(1)}, f32[2,128]{1,0:T(2,128)}, u32[]{:S(2)}) copy-start(f32[2,128]{1,0:T(2,128)} %constant.21.clone.shifts) | copy-start | bytes 3076
  54.4 12.8 %collective-permute-start.4 = (f32[1344,128]{1,0:T(8,128)}, f32[1344,128]{1,0:T(8,128)S(1)}, u32[]{:S(2)}, u32[]{:S(2)}) collective-permute-start(f32[1344,128]{1,0:T(8,128)} %get-tuple-element.19), channel_id=1, source_target_pairs={{0,1},{1,2},{2,3},{3,4},{4,5},{5,6},{6,7},{8,9},{9,10},{10,11},{11... | collective-permute-start | bytes 2064392 | tf_op jit(solution)/shard_map/ppermute | solution.py:367
  59.0 12.3 %collective-permute-start.5 = (f32[1344,128]{1,0:T(8,128)S(1)}, f32[1344,128]{1,0:T(8,128)S(1)}, u32[]{:S(2)}, u32[]{:S(2)}) collective-permute-start(f32[1344,128]{1,0:T(8,128)S(1)} %get-tuple-element.20), channel_id=1, source_target_pairs={{1,0},{2,1},{3,2},{4,3},{5,4},{6,5},{7,6},{9,8},{10,9},{11,10},{12... | collective-permute-start | bytes 2064392 | tf_op jit(solution)/shard_map/ppermute | solution.py:367
  61.5 9.8 %copy-start.6 = (bf16[512,512]{1,0:T(8,128)(2,1)S(1)}, bf16[512,512]{1,0:T(8,128)(2,1)}, u32[]{:S(2)}) copy-start(bf16[512,512]{1,0:T(8,128)(2,1)} %constant.23.clone.low) | copy-start | bytes 1572868
  61.5 9.8 %copy-start.7 = (bf16[512,512]{1,0:T(8,128)(2,1)S(1)}, bf16[512,512]{1,0:T(8,128)(2,1)}, u32[]{:S(2)}) copy-start(bf16[512,512]{1,0:T(8,128)(2,1)} %constant.22.clone.high) | copy-start | bytes 1572868
  78.8 22.2 %copy-start.1 = (f32[2,4,8,1024]{3,2,1,0:T(8,128)S(1)}, f32[2,4,8,1024]{3,2,1,0:T(8,128)}, u32[]{:S(2)}) copy-start(f32[2,4,8,1024]{3,2,1,0:T(8,128)} %state.7) | copy-start | bytes 786436
  78.9 22.2 %copy-start.3 = (f32[2,4,8,1024]{3,2,1,0:T(8,128)S(1)}, f32[2,4,8,1024]{3,2,1,0:T(8,128)}, u32[]{:S(2)}) copy-start(f32[2,4,8,1024]{3,2,1,0:T(8,128)} %adjoint.7) | copy-start | bytes 786436

commit v3 on v2

--- a/solution.py
+++ b/solution.py
@@ -18,6 +18,7 @@
 DEEP = SWEEPS - 1
 SUBLANES = 8
 VMEM_LIMIT = 28 * 1024 * 1024
+WHOLE_VMEM = 60 * 1024 * 1024
 
 
 def transforms(period):
@@ -63,10 +64,19 @@
     return dot(high, high_ref[...]) + (dot(low, high_ref[...]) + dot(high, low_ref[...]))
 
 
-def pack_kernel(own_cols, me, state, adjoint, cond, to_down, to_up, last, first):
+def fetch(sources, targets, sems):
+    copies = [pltpu.make_async_copy(x, y, sems.at[i]) for i, (x, y) in enumerate(zip(sources, targets))]
+    for copy in copies:
+        copy.start()
+    return copies
+
+
+def pack_kernel(own_cols, me, state_far, adjoint_far, cond_far, to_down, to_up, last, first, state, adjoint, cond, sems):
     steps, planes, rows, cols = state.shape
     tiles = cols // LANES
     per_tile = 2 * steps * planes
+    for copy in fetch((state_far, adjoint_far, cond_far), (state, adjoint, cond), sems):
+        copy.wait()
     for out, r in ((to_down, rows - 1), (to_up, 0)):
         for k in range(tiles):
             lanes = pl.ds(k * LANES, LANES)
@@ -92,7 +102,12 @@
     return jnp.concatenate([packed[pl.ds(base + k * stride + at, 1), :] for k in range(tiles)], axis=1)
 
 
-def local_kernel(state, adjoint, source, target, cond, out):
+def local_kernel(*refs):
+    count = 5
+    out, sems = refs[count], refs[-1]
+    state, adjoint, source, target, cond = refs[count + 1 : 2 * count + 1]
+    for copy in fetch(refs[:count], refs[count + 1 : 2 * count + 1], sems):
+        copy.wait()
     steps, planes, rows, cols = state.shape
     row = lax.broadcasted_iota(jnp.int32, (rows, cols), 0)
     col = lax.broadcasted_iota(jnp.int32, (rows, cols), 1)
@@ -137,24 +152,29 @@
                 out[pl.ds(((t * 2 + f) * planes + p) * rows, rows), :] = value
 
 
-def finish_kernel(blocks, partial, state, adjoint, prior, later, top, bottom, cond, out, res, turned):
-    steps, planes, rows, cols = state.shape
+def finish_kernel(shape, place, partial, to_down, to_up, prior, later, top, bottom, out, res, turned):
+    blocks, steps, planes, rows, ends = shape
+    cols = partial.shape[1]
     tiles = cols // LANES
     per_tile = 2 * steps * planes
     row = lax.broadcasted_iota(jnp.int32, (rows, cols), 0)
+    inside = [jnp.where(place[0] == end, 0.0, 1.0) for end in ends]
+    sides = ((0, to_up, top), (rows - 1, to_down, bottom))
     for p in range(planes):
         weights = []
-        for packed, r in ((top, 0), (bottom, rows - 1)):
-            beyond = edge_row(packed, tiles, tiles * per_tile, planes, p)
-            weights.append(jnp.where(row == r, (0.5 * STEP) * (cond[p] + beyond), 0.0))
+        for i, (_, mine, other) in enumerate(sides):
+            here = edge_row(mine, tiles, tiles * per_tile, planes, p)
+            beyond = edge_row(other, tiles, tiles * per_tile, planes, p)
+            weights.append((0.5 * STEP) * (here + beyond * inside[i]))
         for t in range(steps):
-            for f, field in enumerate((state, adjoint)):
+            for f in range(2):
                 at = ((t * 2 + f) * planes + p) * rows
                 edge = (f * steps + t) * planes + p
-                value = field[t, p]
                 total = partial[pl.ds(at, rows), :]
-                for packed, w in zip((top, bottom), weights):
-                    total = total - w * (value - edge_row(packed, tiles, 0, per_tile, edge))
+                for i, (r, mine, other) in enumerate(sides):
+                    here = edge_row(mine, tiles, 0, per_tile, edge)
+                    beyond = edge_row(other, tiles, 0, per_tile, edge)
+                    total = jnp.where(row == r, total - weights[i] * (here - beyond * inside[i]), total)
                 if f == 0 and t == 0:
                     total = total + prior[p]
                 if f == 1 and t == steps - 1:
@@ -174,8 +194,9 @@
     return near + [span - 1 - c for c in near]
 
 
-def forward_kernel(shape, got, high, low, own, up, down, left):
+def forward_kernel(shape, got, high_far, low_far, own, up, down, left, high, low, sems):
     blocks, span, planes, rows = shape
+    copies = fetch((high_far, low_far), (high, low), sems)
     strip = span // (2 * SUBLANES)
     line = planes * span
     cells = planes * rows
@@ -184,6 +205,8 @@
         turned = jnp.concatenate(parts, axis=0).T
         for tf in range(4):
             left[pl.ds(g * cells, cells), pl.ds(tf * LANES, LANES)] = turned[tf * cells : (tf + 1) * cells]
+    for copy in copies:
+        copy.wait()
     spectrum = dot_split(left[...], high, low)
     for g in range(span // 4):
         for pair in range(2):
@@ -343,28 +366,31 @@
                     )
 
 
-def call(kernel, outs, scratch, flops, moved, *args, scalars=0):
+def call(kernel, outs, scratch, flops, moved, *args, places="", limit=VMEM_LIMIT):
+    spaces = {"s": pltpu.SMEM, "h": pltpu.HBM, "v": pltpu.VMEM}
     vmem = pl.BlockSpec(memory_space=pltpu.VMEM)
-    smem = pl.BlockSpec(memory_space=pltpu.SMEM)
     return pl.pallas_call(
         kernel,
         out_shape=outs,
-        in_specs=[smem] * scalars + [vmem] * (len(args) - scalars),
+        in_specs=[pl.BlockSpec(memory_space=spaces[x]) for x in places.ljust(len(args), "v")],
         out_specs=[vmem] * len(outs) if isinstance(outs, list) else vmem,
         scratch_shapes=scratch,
-        compiler_params=pltpu.CompilerParams(vmem_limit_bytes=VMEM_LIMIT),
+        compiler_params=pltpu.CompilerParams(vmem_limit_bytes=limit),
         cost_estimate=pl.CostEstimate(flops=flops, bytes_accessed=moved, transcendentals=0),
     )(*args)
 
 
+def v32(*shape):
+    return pltpu.VMEM(shape, jnp.float32)
+
+
 def f32(*shape):
     return jax.ShapeDtypeStruct(shape, jnp.float32)
 
 
-def shift(block, axis, distance, wrap):
+def shift(block, axis, distance):
     count = lax.axis_size(axis)
-    route = [(i, (i + distance) % count) for i in range(count) if wrap or 0 <= i + distance < count]
-    return lax.ppermute(block, axis, route)
+    return lax.ppermute(block, axis, [(i, (i + distance) % count) for i in range(count)])
 
 
 def body(state, adjoint, source, target, conductivity):
@@ -393,48 +419,60 @@
     to_down, to_up, last, first = call(
         functools.partial(pack_kernel, own_cols),
         [f32(edges, LANES), f32(edges, LANES), f32(planes, rows, cols), f32(planes, rows, cols)],
-        [],
+        [v32(*state.shape), v32(*state.shape), v32(*conductivity.shape), pltpu.SemaphoreType.DMA((3,))],
         10**5,
         10**6,
         me.reshape(1), state, adjoint, conductivity,
-        scalars=1,
-    )
-    top = shift(to_down, "space", 1, False)
-    bottom = shift(to_up, "space", -1, False)
-    prior = shift(last, "tm", 1, True)
-    later = shift(first, "tm", -1, True)
+        places="shhh",
+        limit=WHOLE_VMEM,
+    )
+    top = shift(to_down, "space", 1)
+    bottom = shift(to_up, "space", -1)
+    prior = shift(last, "tm", 1)
+    later = shift(first, "tm", -1)
     partial = call(
         local_kernel,
         f32(LANES, cols),
-        [],
+        [v32(*state.shape)] * 4 + [v32(*conductivity.shape), pltpu.SemaphoreType.DMA((5,))],
         10**7,
         3 * 10**6,
         state, adjoint, source, target, conductivity,
-    )
+        places="hhhhh",
+        limit=WHOLE_VMEM,
+    )
+    place = lax.axis_index("space")
     sent = call(
-        functools.partial(finish_kernel, blocks),
+        functools.partial(finish_kernel, (blocks, steps, planes, rows, (0, lax.axis_size("space") - 1))),
         f32(blocks, span, LANES),
-        [pltpu.VMEM((LANES, cols), jnp.float32), pltpu.VMEM((cols + 2 * WIDE, LANES), jnp.float32)],
+        [v32(LANES, cols), v32(cols + 2 * WIDE, LANES)],
         10**7,
         3 * 10**6,
-        partial, state, adjoint, prior, later, top, bottom, conductivity,
+        place.reshape(1), partial, to_down, to_up, prior, later, top, bottom,
+        places="s",
     )
     got = lax.all_to_all(sent, "tm", 0, 0, tiled=True).reshape(blocks * span, LANES)
     own, up, down = call(
         functools.partial(forward_kernel, (blocks, span, planes, rows)),
         [f32(rows * line, LANES), f32(DEEP * line, LANES), f32(DEEP * line, LANES)],
-        [pltpu.VMEM((span // 4 * planes * rows, 4 * LANES), jnp.float32)],
+        [
+            v32(span // 4 * planes * rows, 4 * LANES),
+            pltpu.VMEM(forward_high.shape, jnp.bfloat16),
+            pltpu.VMEM(forward_low.shape, jnp.bfloat16),
+            pltpu.SemaphoreType.DMA((2,)),
+        ],
         6 * 10**8,
         4 * 10**6,
         got, forward_high, forward_low,
-    )
-    above = shift(down, "space", 1, False)
-    below = shift(up, "space", -1, False)
-
-    def unpack(packed):
-        return packed[edges - planes * rows :].reshape(planes, rows, LANES)[..., :span]
-
-    kappa = jnp.concatenate([unpack(top), unpack(to_up), unpack(bottom)], axis=1)
+        places="vhh",
+    )
+    above = shift(down, "space", 1)
+    below = shift(up, "space", -1)
+
+    def unpack(packed, end):
+        rim = packed[edges - planes * rows :].reshape(planes, rows, LANES)[..., :span]
+        return jnp.where(place == end, 0.0, rim)
+
+    kappa = jnp.concatenate([unpack(top, 0), unpack(to_up, -1), unpack(bottom, lax.axis_size("space") - 1)], axis=1)
     kappa = jnp.stack([kappa[..., : span // 2], kappa[..., : span // 2 - 1 : -1]], axis=2)
     kappa = kappa.reshape(planes, 3 * rows, 2, SUBLANES, strip).transpose(1, 3, 2, 0, 4).reshape(3 * rows, SUBLANES, 2 * count)
     kappa = jnp.pad(kappa, ((0, 0), (0, 0), (0, LANES - 2 * count)))
@@ -447,7 +485,7 @@
             f32(tall, count, *tile),
             f32(tall, count, *tile),
         ],
-        [pltpu.VMEM((3 * rows, count, *tile), jnp.float32)],
+        [v32(3 * rows, count, *tile)],
         10**9,
         10**7,
         kappa, np.tile(shifts.reshape(2, 2, -1)[:, :1], (1, 2, 1)).reshape(2, LANES),
@@ -456,10 +494,10 @@
         functools.partial(sweep_kernel, (blocks, own_cols, planes, strip)),
         f32(blocks * own_cols, LANES),
         [
-            pltpu.VMEM((tall, 2 * count, *tile), jnp.float32),
-            pltpu.VMEM((tall * line, LANES), jnp.float32),
-            pltpu.VMEM((tall * line, LANES), jnp.float32),
-            pltpu.VMEM((own_cols // 4 * planes * rows, 4 * LANES), jnp.float32),
+            v32(tall, 2 * count, *tile),
+            v32(tall * line, LANES),
+            v32(tall * line, LANES),
+            v32(own_cols // 4 * planes * rows, 4 * LANES),
         ],
         10**9,
         6 * 10**6,

time: 103 us -> 94.8 us (0.920)
  starting transfers between devices: 26.3 us -> 17.8 us
  local copies, waits for them, and re-layouts: 7.11 us -> 2.17 us
  Pallas kernels: 17.2 us -> 21.4 us
    ppermute x6, starting transfers between devices: 14.3 us -> 5.83 us  [shift(): lax.ppermute(block, axis, [(i, (i + distance) % count) for i in range(cou...]
    unnamed x29, local copies, waits for them, and re-layouts: 6.96 us -> 2.02 us
    pallas_call x7, Pallas kernels: 17.2 us -> 21.4 us  [call(): pl.pallas_call(kernel, out_shape=outs, in_specs=[pl.BlockSpec(memory_spac...]
    ppermute x6, waiting for transfers between devices: 5.87 us -> 6.95 us  [shift(): lax.ppermute(block, axis, [(i, (i + distance) % count) for i in range(cou...]
  transfers between devices with their start and end apart: 7 -> 7, of which waited for: 4 -> 4; matrix products, arithmetic and copies ran while one was open for 1% -> 2% of each run, Pallas kernels for 5% -> 8%
where the time goes in v3:
time: 94.8 us; the launch traced here: 93.9 us
  waiting for transfers between devices  28.4 us (30%)
  blocking collectives  22.4 us (24%)
  Pallas kernels  21.4 us (23%)
  starting transfers between devices  17.8 us (19%)
  local copies, waits for them, and re-layouts  2.17 us (2%)
  other arithmetic  0.95 us (1%)
    all_to_all x1, blocking collectives, body(): got_back = lax.all_to_all(back, 'tm', 0, 0, tiled=True)  22.4 us
    all_to_all x1, waiting for transfers between devices, body(): lax.all_to_all(sent, 'tm', 0, 0, tiled=True).reshape(blocks * span, LANES)  21.4 us
    pallas_call x7, Pallas kernels, call(): pl.pallas_call(kernel, out_shape=outs, in_specs=[pl.BlockSpec(memory_spac...  21.4 us
    all_to_all x1, starting transfers between devices, body(): lax.all_to_all(sent, 'tm', 0, 0, tiled=True).reshape(blocks * span, LANES)  12 us
    ppermute x6, waiting for transfers between devices, shift(): lax.ppermute(block, axis, [(i, (i + distance) % count) for i in range(cou...  6.95 us
    ppermute x6, starting transfers between devices, shift(): lax.ppermute(block, axis, [(i, (i + distance) % count) for i in range(cou...  5.83 us
    unnamed x29, local copies, waits for them, and re-layouts  2.02 us
  transfers between devices with their start and end apart: 7, of which 4 were waited for; matrix products, arithmetic and copies ran while one was open for 2% of the time, Pallas kernels for 8%

profile of v3, /device:TPU:41, one launch (start us, length us, event | category | flops | bytes accessed | tf_op | source)
XLA Modules:
  0.0 93.9 jit_solution(17215087783250140804)
XLA Ops:
  0.6 2.0 %shard_map.114 = (f32[192,128]{1,0:T(8,128)}, f32[192,128]{1,0:T(8,128)}, f32[4,8,1024]{2,1,0:T(8,128)}, f32[4,8,1024]{2,1,0:T(8,128)}) custom-call(s32[1]{0:T(128)} %bitcast.1.me, f32[2,4,8,1024]{3,2,1,0:T(8,128)} %state.1, f32[2,4,8,1024]{3,2,1,0:T(8,128)} %adjoint.1, f32[4,8,1024]{2,1,0:T(8,128)} %cond_far.1), custom_call_target="tpu_custom_call" | custom-call | flops 100000 | bytes 1000000 | tf_op jit(solution)/shard_map/pallas_call | solution.py:372
  2.7 1.7 %collective-permute-start = (f32[4,8,1024]{2,1,0:T(8,128)}, f32[4,8,1024]{2,1,0:T(8,128)S(1)}, u32[]{:S(2)}, u32[]{:S(2)}) collective-permute-start(f32[4,8,1024]{2,1,0:T(8,128)} %get-tuple-element.16), channel_id=1, source_target_pairs={{0,8},{8,16},{16,24},{24,32},{32,40},{40,48},{48,56},{56,64},{64,7... | collective-permute-start | bytes 393224 | tf_op jit(solution)/shard_map/ppermute | solution.py:393
  4.4 2.2 %collective-permute-start.2 = (f32[192,128]{1,0:T(8,128)}, f32[192,128]{1,0:T(8,128)S(1)}, u32[]{:S(2)}, u32[]{:S(2)}) collective-permute-start(f32[192,128]{1,0:T(8,128)} %get-tuple-element.14.to_down), channel_id=1, source_target_pairs={{0,1},{1,2},{2,3},{3,4},{4,5},{5,6},{6,7},{7,0},{8,9},{9,10},{10,1... | collective-permute-start | bytes 294920 | tf_op jit(solution)/shard_map/ppermute | solution.py:393
  6.6 0.0 collective-permute-start.3
  6.6 2.7 %shard_map.113.partial = f32[128,1024]{1,0:T(8,128)} custom-call(f32[2,4,8,1024]{3,2,1,0:T(8,128)} %state.1, f32[2,4,8,1024]{3,2,1,0:T(8,128)} %adjoint.1, f32[2,4,8,1024]{3,2,1,0:T(8,128)} %refs_2_.1, f32[2,4,8,1024]{3,2,1,0:T(8,128)} %refs_3_.1, f32[4,8,1024]{2,1,0:T(8,128)} %cond_far.1), custom_call_target="tpu_custom_call" | custom-call | flops 10000000 | bytes 3000000 | tf_op jit(solution)/shard_map/pallas_call | solution.py:372
  9.3 1.6 %collective-permute-done.3.bottom = f32[192,128]{1,0:T(8,128)S(1)} collective-permute-done((f32[192,128]{1,0:T(8,128)}, f32[192,128]{1,0:T(8,128)S(1)}, u32[]{:S(2)}, u32[]{:S(2)}) %collective-permute-start.3) | collective-permute-done | bytes 98336 | tf_op jit(solution)/shard_map/ppermute | solution.py:393
  10.9 0.0 collective-permute-done.prior
  10.9 1.0 %copy-done.2 = f32[128,1024]{1,0:T(8,128)S(1)} copy-done((f32[128,1024]{1,0:T(8,128)S(1)}, f32[128,1024]{1,0:T(8,128)}, u32[]{:S(2)}) %copy-start.2) | copy-done | bytes 524312
  11.9 1.2 %shard_map.115 = f32[32,48,128]{2,1,0:T(8,128)} custom-call(s32[1]{0:T(128)} %bitcast.place, f32[128,1024]{1,0:T(8,128)S(1)} %copy-done.2, f32[192,128]{1,0:T(8,128)S(1)} %copy-done.6, f32[192,128]{1,0:T(8,128)S(1)} %copy-done.5, f32[4,8,1024]{2,1,0:T(8,128)S(1)} %collective-permute-done.prior, f32[4,8,1024]{2,1,0:T(8,128)S(1)} %collective-permute-done.1.later, ...), custom_call_target="tpu_custom_call" | custom-call | flops 10000000 | bytes 3000000 | tf_op jit(solution)/shard_map/pallas_call | solution.py:372
  13.1 12.0 %all-to-all-start = ((f32[32,48,128]{2,1,0:T(8,128)}), f32[32,48,128]{2,1,0:T(8,128)S(1)}, u32[]{:S(2)}, u32[]{:S(2)}) async-start(f32[32,48,128]{2,1,0:T(8,128)} %shard_map.115), calls=%async_computation | async-start | bytes 1572864 | tf_op jit(solution)/shard_map/all_to_all | solution.py:453
  25.1 0.1 copy.18
  25.2 0.7 copy.17
  26.0 0.1 copy.19
  26.1 0.7 broadcast_select_fusion
  26.8 21.4 %all-to-all-done = f32[32,48,128]{2,1,0:T(8,128)S(1)} async-done(((f32[32,48,128]{2,1,0:T(8,128)}), f32[32,48,128]{2,1,0:T(8,128)S(1)}, u32[]{:S(2)}, u32[]{:S(2)}) %all-to-all-start) | async-done | bytes 786464 | tf_op jit(solution)/shard_map/all_to_all | solution.py:453
  48.2 0.0 copy-start.12
  48.3 2.5 %shard_map.116 = (f32[1536,128]{1,0:T(8,128)S(1)}, f32[1344,128]{1,0:T(8,128)S(1)}, f32[1344,128]{1,0:T(8,128)}) custom-call(f32[1536,128]{1,0:T(8,128)S(1)} %bitcast.24, bf16[512,512]{1,0:T(8,128)(2,1)S(1)} %copy-done.8, bf16[512,512]{1,0:T(8,128)(2,1)S(1)} %copy-done.7), custom_call_target="tpu_custom_call" | custom-call | flops 600000000 | bytes 4000000 | tf_op jit(solution)/shard_map/pallas_call | solution.py:372
  50.8 0.0 copy-start.9
  50.8 1.9 %collective-permute-start.4 = (f32[1344,128]{1,0:T(8,128)}, f32[1344,128]{1,0:T(8,128)S(1)}, u32[]{:S(2)}, u32[]{:S(2)}) collective-permute-start(f32[1344,128]{1,0:T(8,128)} %get-tuple-element.19), channel_id=1, source_target_pairs={{0,1},{1,2},{2,3},{3,4},{4,5},{5,6},{6,7},{7,0},{8,9},{9,10},{10,1... | collective-permute-start | bytes 2064392 | tf_op jit(solution)/shard_map/ppermute | solution.py:393
  52.7 0.0 collective-permute-start.5
  52.7 0.2 pad_maximum_fusion
  53.0 0.1 copy.16
  53.1 0.0 copy-start.3
  53.1 0.0 copy-start.4
  53.1 4.5 %shard_map.117 = (f32[22,12,8,128]{3,2,1,0:T(8,128)S(1)}, f32[22,16,8,128]{3,2,1,0:T(8,128)S(1)}, f32[22,9,8,128]{3,2,1,0:T(8,128)S(1)}, f32[22,12,8,128]{3,2,1,0:T(8,128)S(1)}, f32[22,12,8,128]{3,2,1,0:T(8,128)S(1)}) custom-call(f32[24,8,128]{2,1,0:T(8,128)S(1)} %pad.4.kappa, f32[2,128]{1,0:T(2,128)S(1)} %copy-done.9), custom_call_target="tpu_custom_call" | custom-call | flops 1000000000 | bytes 10000000 | tf_op jit(solution)/shard_map/pallas_call | solution.py:372
  57.6 3.2 %collective-permute-done.4 = f32[1344,128]{1,0:T(8,128)S(1)} collective-permute-done((f32[1344,128]{1,0:T(8,128)}, f32[1344,128]{1,0:T(8,128)S(1)}, u32[]{:S(2)}, u32[]{:S(2)}) %collective-permute-start.4) | collective-permute-done | bytes 688160 | tf_op jit(solution)/shard_map/ppermute | solution.py:393
  60.9 2.2 %collective-permute-done.5 = f32[1344,128]{1,0:T(8,128)S(1)} collective-permute-done((f32[1344,128]{1,0:T(8,128)S(1)}, f32[1344,128]{1,0:T(8,128)S(1)}, u32[]{:S(2)}, u32[]{:S(2)}) %collective-permute-start.5) | collective-permute-done | bytes 688160 | tf_op jit(solution)/shard_map/ppermute | solution.py:393
  63.0 7.5 %shard_map.118 = f32[1024,128]{1,0:T(8,128)S(1)} custom-call(f32[8,24,8,128]{3,2,1,0:T(8,128)S(1)} %bitcast.25, f32[7,24,8,128]{3,2,1,0:T(8,128)S(1)} %bitcast.26, f32[7,24,8,128]{3,2,1,0:T(8,128)S(1)} %bitcast.27, f32[22,12,8,128]{3,2,1,0:T(8,128)S(1)} %get-tuple-element.21.w_row, f32[22,16,8,128]{3,2,1,0:T(8,128)S(1)} %get-tuple-element.22.w_col, ...), custom_call_target="tpu_custom_call" | custom-call | flops 1000000000 | bytes 6000000 | tf_op jit(solution)/shard_map/pallas_call | solution.py:372
  70.6 0.0 copy-start
  70.6 0.0 copy-start.1
  70.6 22.4 %all_to_all.16 = f32[32,32,128]{2,1,0:T(8,128)S(1)} all-to-all(f32[32,32,128]{2,1,0:T(8,128)S(1)} %bitcast.23), channel_id=1, replica_groups=mesh['tm'=32,'space'=8] {'tm'}, dimensions={0} | all-to-all | bytes 1048576 | tf_op jit(solution)/shard_map/all_to_all | solution.py:507
  93.0 1.0 %shard_map.119 = (f32[2,4,8,1024]{3,2,1,0:T(8,128)}, f32[2,4,8,1024]{3,2,1,0:T(8,128)}) custom-call(f32[1024,128]{1,0:T(8,128)S(1)} %bitcast.22, f32[2,4,8,1024]{3,2,1,0:T(8,128)S(1)} %copy-done, f32[2,4,8,1024]{3,2,1,0:T(8,128)S(1)} %copy-done.1), custom_call_target="tpu_custom_call" | custom-call | flops 1000000 | bytes 2000000 | tf_op jit(solution)/shard_map/pallas_call | solution.py:372
  (31 shorter events, 0.1 us)
Async XLA Ops:
  2.6 8.2 %copy-start.5 = (f32[192,128]{1,0:T(8,128)S(1)}, f32[192,128]{1,0:T(8,128)}, u32[]{:S(2)}) copy-start(f32[192,128]{1,0:T(8,128)} %get-tuple-element.15.to_up) | copy-start | bytes 294916
  2.6 8.2 %copy-start.6 = (f32[192,128]{1,0:T(8,128)S(1)}, f32[192,128]{1,0:T(8,128)}, u32[]{:S(2)}) copy-start(f32[192,128]{1,0:T(8,128)} %get-tuple-element.14.to_down) | copy-start | bytes 294916
  2.7 8.2 %collective-permute-start = (f32[4,8,1024]{2,1,0:T(8,128)}, f32[4,8,1024]{2,1,0:T(8,128)S(1)}, u32[]{:S(2)}, u32[]{:S(2)}) collective-permute-start(f32[4,8,1024]{2,1,0:T(8,128)} %get-tuple-element.16), channel_id=1, source_target_pairs={{0,8},{8,16},{16,24},{24,32},{32,40},{40,48},{48,56},{56,64},{64,7... | collective-permute-start | bytes 393224 | tf_op jit(solution)/shard_map/ppermute | solution.py:393
  4.4 6.5 %collective-permute-start.1 = (f32[4,8,1024]{2,1,0:T(8,128)}, f32[4,8,1024]{2,1,0:T(8,128)S(1)}, u32[]{:S(2)}, u32[]{:S(2)}) collective-permute-start(f32[4,8,1024]{2,1,0:T(8,128)} %get-tuple-element.17), channel_id=1, source_target_pairs={{0,248},{8,0},{16,8},{24,16},{32,24},{40,32},{48,40},{56,48},{64,5... | collective-permute-start | bytes 393224 | tf_op jit(solution)/shard_map/ppermute | solution.py:393
  4.4 4.9 %collective-permute-start.2 = (f32[192,128]{1,0:T(8,128)}, f32[192,128]{1,0:T(8,128)S(1)}, u32[]{:S(2)}, u32[]{:S(2)}) collective-permute-start(f32[192,128]{1,0:T(8,128)} %get-tuple-element.14.to_down), channel_id=1, source_target_pairs={{0,1},{1,2},{2,3},{3,4},{4,5},{5,6},{6,7},{7,0},{8,9},{9,10},{10,1... | collective-permute-start | bytes 294920 | tf_op jit(solution)/shard_map/ppermute | solution.py:393
  6.6 4.3 %collective-permute-start.3 = (f32[192,128]{1,0:T(8,128)}, f32[192,128]{1,0:T(8,128)S(1)}, u32[]{:S(2)}, u32[]{:S(2)}) collective-permute-start(f32[192,128]{1,0:T(8,128)} %get-tuple-element.15.to_up), channel_id=1, source_target_pairs={{0,7},{1,0},{2,1},{3,2},{4,3},{5,4},{6,5},{7,6},{8,15},{9,8},{10,9... | collective-permute-start | bytes 294920 | tf_op jit(solution)/shard_map/ppermute | solution.py:393
  10.9 1.0 %copy-start.2 = (f32[128,1024]{1,0:T(8,128)S(1)}, f32[128,1024]{1,0:T(8,128)}, u32[]{:S(2)}) copy-start(f32[128,1024]{1,0:T(8,128)} %shard_map.113.partial) | copy-start | bytes 1572868
  13.1 35.1 %copy-start.7 = (bf16[512,512]{1,0:T(8,128)(2,1)S(1)}, bf16[512,512]{1,0:T(8,128)(2,1)}, u32[]{:S(2)}) copy-start(bf16[512,512]{1,0:T(8,128)(2,1)} %constant.29.clone.low_far) | copy-start | bytes 1572868
  13.1 35.1 %copy-start.8 = (bf16[512,512]{1,0:T(8,128)(2,1)S(1)}, bf16[512,512]{1,0:T(8,128)(2,1)}, u32[]{:S(2)}) copy-start(bf16[512,512]{1,0:T(8,128)(2,1)} %constant.28.clone.high_far) | copy-start | bytes 1572868
  13.1 35.1 %all-to-all-start = ((f32[32,48,128]{2,1,0:T(8,128)}), f32[32,48,128]{2,1,0:T(8,128)S(1)}, u32[]{:S(2)}, u32[]{:S(2)}) async-start(f32[32,48,128]{2,1,0:T(8,128)} %shard_map.115), calls=%async_computation | async-start | bytes 1572864 | tf_op jit(solution)/shard_map/all_to_all | solution.py:453
  48.2 4.4 %copy-start.10 = (f32[4,8,48]{1,0,2:T(4,128)S(1)}, f32[4,8,48]{1,0,2:T(4,128)}, u32[]{:S(2)}) copy-start(f32[4,8,48]{1,0,2:T(4,128)} %copy.17) | copy-start | bytes 18436
  48.2 4.5 %copy-start.11 = (f32[4,8,48]{1,0,2:T(4,128)S(1)}, f32[4,8,48]{1,0,2:T(4,128)}, u32[]{:S(2)}) copy-start(f32[4,8,48]{1,0,2:T(4,128)} %get-tuple-element.28) | copy-start | bytes 18436
  48.2 4.5 %copy-start.12 = (f32[4,8,48]{1,0,2:T(4,128)S(1)}, f32[4,8,48]{1,0,2:T(4,128)}, u32[]{:S(2)}) copy-start(f32[4,8,48]{1,0,2:T(4,128)} %get-tuple-element.29) | copy-start | bytes 18436
  50.8 2.3 %copy-start.9 = (f32[2,128]{1,0:T(2,128)S(1)}, f32[2,128]{1,0:T(2,128)}, u32[]{:S(2)}) copy-start(f32[2,128]{1,0:T(2,128)} %constant.30.clone.shifts) | copy-start | bytes 3076
  50.8 10.1 %collective-permute-start.4 = (f32[1344,128]{1,0:T(8,128)}, f32[1344,128]{1,0:T(8,128)S(1)}, u32[]{:S(2)}, u32[]{:S(2)}) collective-permute-start(f32[1344,128]{1,0:T(8,128)} %get-tuple-element.19), channel_id=1, source_target_pairs={{0,1},{1,2},{2,3},{3,4},{4,5},{5,6},{6,7},{7,0},{8,9},{9,10},{10,1... | collective-permute-start | bytes 2064392 | tf_op jit(solution)/shard_map/ppermute | solution.py:393
  52.7 10.4 %collective-permute-start.5 = (f32[1344,128]{1,0:T(8,128)S(1)}, f32[1344,128]{1,0:T(8,128)S(1)}, u32[]{:S(2)}, u32[]{:S(2)}) collective-permute-start(f32[1344,128]{1,0:T(8,128)S(1)} %get-tuple-element.20), channel_id=1, source_target_pairs={{0,7},{1,0},{2,1},{3,2},{4,3},{5,4},{6,5},{7,6},{8,15},{9,8},{10,9... | collective-permute-start | bytes 2064392 | tf_op jit(solution)/shard_map/ppermute | solution.py:393
  53.1 9.9 %copy-start.3 = (bf16[512,512]{1,0:T(8,128)(2,1)S(1)}, bf16[512,512]{1,0:T(8,128)(2,1)}, u32[]{:S(2)}) copy-start(bf16[512,512]{1,0:T(8,128)(2,1)} %constant.32.clone.low) | copy-start | bytes 1572868
  53.1 9.9 %copy-start.4 = (bf16[512,512]{1,0:T(8,128)(2,1)S(1)}, bf16[512,512]{1,0:T(8,128)(2,1)}, u32[]{:S(2)}) copy-start(bf16[512,512]{1,0:T(8,128)(2,1)} %constant.31.clone.high) | copy-start | bytes 1572868
  70.6 22.4 %copy-start = (f32[2,4,8,1024]{3,2,1,0:T(8,128)S(1)}, f32[2,4,8,1024]{3,2,1,0:T(8,128)}, u32[]{:S(2)}) copy-start(f32[2,4,8,1024]{3,2,1,0:T(8,128)} %state.1) | copy-start | bytes 786436
  70.6 22.4 %copy-start.1 = (f32[2,4,8,1024]{3,2,1,0:T(8,128)S(1)}, f32[2,4,8,1024]{3,2,1,0:T(8,128)}, u32[]{:S(2)}) copy-start(f32[2,4,8,1024]{3,2,1,0:T(8,128)} %adjoint.1) | copy-start | bytes 786436

commit v4 on v3

--- a/solution.py
+++ b/solution.py
@@ -19,6 +19,7 @@
 SUBLANES = 8
 VMEM_LIMIT = 28 * 1024 * 1024
 WHOLE_VMEM = 60 * 1024 * 1024
+PACK_VMEM = 54682 * 1024
 
 
 def transforms(period):
@@ -424,7 +425,7 @@
         10**6,
         me.reshape(1), state, adjoint, conductivity,
         places="shhh",
-        limit=WHOLE_VMEM,
+        limit=PACK_VMEM,
     )
     top = shift(to_down, "space", 1)
     bottom = shift(to_up, "space", -1)

time: 94.8 us -> 94 us (level)
    unnamed x29 -> x25, local copies, waits for them, and re-layouts: 2.02 us -> 2.01 us
where the time goes in v4:
time: 94 us; the launch traced here: 93.4 us
  waiting for transfers between devices  28.7 us (31%)
  blocking collectives  22.8 us (24%)
  Pallas kernels  20.7 us (22%)
  starting transfers between devices  17.2 us (18%)
  local copies, waits for them, and re-layouts  2.17 us (2%)
  other arithmetic  0.95 us (1%)
    all_to_all x1, blocking collectives, body(): got_back = lax.all_to_all(back, 'tm', 0, 0, tiled=True)  22.8 us
    all_to_all x1, waiting for transfers between devices, body(): lax.all_to_all(sent, 'tm', 0, 0, tiled=True).reshape(blocks * span, LANES)  22 us
    pallas_call x7, Pallas kernels, call(): pl.pallas_call(kernel, out_shape=outs, in_specs=[pl.BlockSpec(memory_spac...  20.7 us
    all_to_all x1, starting transfers between devices, body(): lax.all_to_all(sent, 'tm', 0, 0, tiled=True).reshape(blocks * span, LANES)  12 us
    ppermute x6, waiting for transfers between devices, shift(): lax.ppermute(block, axis, [(i, (i + distance) % count) for i in range(cou...  6.74 us
    ppermute x6, starting transfers between devices, shift(): lax.ppermute(block, axis, [(i, (i + distance) % count) for i in range(cou...  5.21 us
    unnamed x25, local copies, waits for them, and re-layouts  2.01 us
  transfers between devices with their start and end apart: 7, of which 4 were waited for; matrix products, arithmetic and copies ran while one was open for 2% of the time, Pallas kernels for 8%

profile of v4, /device:TPU:41, one launch (start us, length us, event | category | flops | bytes accessed | tf_op | source)
XLA Modules:
  0.0 93.4 jit_solution(3623709170667671797)
XLA Ops:
  0.6 1.3 %shard_map.114 = (f32[192,128]{1,0:T(8,128)S(1)}, f32[192,128]{1,0:T(8,128)S(1)}, f32[4,8,1024]{2,1,0:T(8,128)S(1)}, f32[4,8,1024]{2,1,0:T(8,128)S(1)}) custom-call(s32[1]{0:T(128)} %bitcast.1.me, f32[2,4,8,1024]{3,2,1,0:T(8,128)} %state.1, f32[2,4,8,1024]{3,2,1,0:T(8,128)} %adjoint.1, f32[4,8,1024]{2,1,0:T(8,128)} %cond_far.1), custom_call_target="tpu_custom_call" | custom-call | flops 100000 | bytes 1000000 | tf_op jit(solution)/shard_map/pallas_call | solution.py:373
  2.0 1.7 %collective-permute-start = (f32[4,8,1024]{2,1,0:T(8,128)S(1)}, f32[4,8,1024]{2,1,0:T(8,128)S(1)}, u32[]{:S(2)}, u32[]{:S(2)}) collective-permute-start(f32[4,8,1024]{2,1,0:T(8,128)S(1)} %get-tuple-element.16), channel_id=1, source_target_pairs={{0,8},{8,16},{16,24},{24,32},{32,40},{40,48},{48,56},{56,64},{64,7... | collective-permute-start | bytes 393224 | tf_op jit(solution)/shard_map/ppermute | solution.py:394
  3.7 0.0 collective-permute-start.1
  3.7 2.2 %collective-permute-start.2 = (f32[192,128]{1,0:T(8,128)S(1)}, f32[192,128]{1,0:T(8,128)S(1)}, u32[]{:S(2)}, u32[]{:S(2)}) collective-permute-start(f32[192,128]{1,0:T(8,128)S(1)} %get-tuple-element.14.to_down), channel_id=1, source_target_pairs={{0,1},{1,2},{2,3},{3,4},{4,5},{5,6},{6,7},{7,0},{8,9},{9,10},{10,1... | collective-permute-start | bytes 294920 | tf_op jit(solution)/shard_map/ppermute | solution.py:394
  5.9 0.0 collective-permute-start.3
  5.9 2.7 %shard_map.113.partial = f32[128,1024]{1,0:T(8,128)} custom-call(f32[2,4,8,1024]{3,2,1,0:T(8,128)} %state.1, f32[2,4,8,1024]{3,2,1,0:T(8,128)} %adjoint.1, f32[2,4,8,1024]{3,2,1,0:T(8,128)} %refs_2_.1, f32[2,4,8,1024]{3,2,1,0:T(8,128)} %refs_3_.1, f32[4,8,1024]{2,1,0:T(8,128)} %cond_far.1), custom_call_target="tpu_custom_call" | custom-call | flops 10000000 | bytes 3000000 | tf_op jit(solution)/shard_map/pallas_call | solution.py:373
  8.6 0.0 collective-permute-done.2.top
  8.6 1.4 %collective-permute-done.3.bottom = f32[192,128]{1,0:T(8,128)S(1)} collective-permute-done((f32[192,128]{1,0:T(8,128)S(1)}, f32[192,128]{1,0:T(8,128)S(1)}, u32[]{:S(2)}, u32[]{:S(2)}) %collective-permute-start.3) | collective-permute-done | bytes 98336 | tf_op jit(solution)/shard_map/ppermute | solution.py:394
  10.0 1.0 %copy-done.2 = f32[128,1024]{1,0:T(8,128)S(1)} copy-done((f32[128,1024]{1,0:T(8,128)S(1)}, f32[128,1024]{1,0:T(8,128)}, u32[]{:S(2)}) %copy-start.2) | copy-done | bytes 524312
  11.0 1.2 %shard_map.115 = f32[32,48,128]{2,1,0:T(8,128)} custom-call(s32[1]{0:T(128)} %bitcast.place, f32[128,1024]{1,0:T(8,128)S(1)} %copy-done.2, f32[192,128]{1,0:T(8,128)S(1)} %get-tuple-element.14.to_down, f32[192,128]{1,0:T(8,128)S(1)} %get-tuple-element.15.to_up, f32[4,8,1024]{2,1,0:T(8,128)S(1)} %collective-permute-done.prior, ...), custom_call_target="tpu_custom_call" | custom-call | flops 10000000 | bytes 3000000 | tf_op jit(solution)/shard_map/pallas_call | solution.py:373
  12.2 12.0 %all-to-all-start = ((f32[32,48,128]{2,1,0:T(8,128)}), f32[32,48,128]{2,1,0:T(8,128)S(1)}, u32[]{:S(2)}, u32[]{:S(2)}) async-start(f32[32,48,128]{2,1,0:T(8,128)} %shard_map.115), calls=%async_computation | async-start | bytes 1572864 | tf_op jit(solution)/shard_map/all_to_all | solution.py:454
  24.2 0.1 copy.18
  24.3 0.7 copy.17
  25.1 0.1 copy.19
  25.2 0.7 broadcast_select_fusion
  25.9 22.0 %all-to-all-done = f32[32,48,128]{2,1,0:T(8,128)S(1)} async-done(((f32[32,48,128]{2,1,0:T(8,128)}), f32[32,48,128]{2,1,0:T(8,128)S(1)}, u32[]{:S(2)}, u32[]{:S(2)}) %all-to-all-start) | async-done | bytes 786464 | tf_op jit(solution)/shard_map/all_to_all | solution.py:454
  47.9 0.0 copy-start.10
  47.9 2.5 %shard_map.116 = (f32[1536,128]{1,0:T(8,128)S(1)}, f32[1344,128]{1,0:T(8,128)S(1)}, f32[1344,128]{1,0:T(8,128)}) custom-call(f32[1536,128]{1,0:T(8,128)S(1)} %bitcast.24, bf16[512,512]{1,0:T(8,128)(2,1)S(1)} %copy-done.6, bf16[512,512]{1,0:T(8,128)(2,1)S(1)} %copy-done.5), custom_call_target="tpu_custom_call" | custom-call | flops 600000000 | bytes 4000000 | tf_op jit(solution)/shard_map/pallas_call | solution.py:373
  50.5 0.0 copy-start.7
  50.5 1.2 %collective-permute-start.4 = (f32[1344,128]{1,0:T(8,128)}, f32[1344,128]{1,0:T(8,128)S(1)}, u32[]{:S(2)}, u32[]{:S(2)}) collective-permute-start(f32[1344,128]{1,0:T(8,128)} %get-tuple-element.19), channel_id=1, source_target_pairs={{0,1},{1,2},{2,3},{3,4},{4,5},{5,6},{6,7},{7,0},{8,9},{9,10},{10,1... | collective-permute-start | bytes 2064392 | tf_op jit(solution)/shard_map/ppermute | solution.py:394
  51.8 0.2 pad_maximum_fusion
  52.0 0.1 copy.16
  52.2 0.0 copy-start.3
  52.2 0.0 copy-start.4
  52.2 4.5 %shard_map.117 = (f32[22,12,8,128]{3,2,1,0:T(8,128)S(1)}, f32[22,16,8,128]{3,2,1,0:T(8,128)S(1)}, f32[22,9,8,128]{3,2,1,0:T(8,128)S(1)}, f32[22,12,8,128]{3,2,1,0:T(8,128)S(1)}, f32[22,12,8,128]{3,2,1,0:T(8,128)S(1)}) custom-call(f32[24,8,128]{2,1,0:T(8,128)S(1)} %pad.4.kappa, f32[2,128]{1,0:T(2,128)S(1)} %copy-done.7), custom_call_target="tpu_custom_call" | custom-call | flops 1000000000 | bytes 10000000 | tf_op jit(solution)/shard_map/pallas_call | solution.py:373
  56.7 3.2 %collective-permute-done.4 = f32[1344,128]{1,0:T(8,128)S(1)} collective-permute-done((f32[1344,128]{1,0:T(8,128)}, f32[1344,128]{1,0:T(8,128)S(1)}, u32[]{:S(2)}, u32[]{:S(2)}) %collective-permute-start.4) | collective-permute-done | bytes 688160 | tf_op jit(solution)/shard_map/ppermute | solution.py:394
  59.9 2.2 %collective-permute-done.5 = f32[1344,128]{1,0:T(8,128)S(1)} collective-permute-done((f32[1344,128]{1,0:T(8,128)S(1)}, f32[1344,128]{1,0:T(8,128)S(1)}, u32[]{:S(2)}, u32[]{:S(2)}) %collective-permute-start.5) | collective-permute-done | bytes 688160 | tf_op jit(solution)/shard_map/ppermute | solution.py:394
  62.1 7.5 %shard_map.118 = f32[1024,128]{1,0:T(8,128)S(1)} custom-call(f32[8,24,8,128]{3,2,1,0:T(8,128)S(1)} %bitcast.25, f32[7,24,8,128]{3,2,1,0:T(8,128)S(1)} %bitcast.26, f32[7,24,8,128]{3,2,1,0:T(8,128)S(1)} %bitcast.27, f32[22,12,8,128]{3,2,1,0:T(8,128)S(1)} %get-tuple-element.21.w_row, f32[22,16,8,128]{3,2,1,0:T(8,128)S(1)} %get-tuple-element.22.w_col, ...), custom_call_target="tpu_custom_call" | custom-call | flops 1000000000 | bytes 6000000 | tf_op jit(solution)/shard_map/pallas_call | solution.py:373
  69.6 0.0 copy-start
  69.6 0.0 copy-start.1
  69.6 22.8 %all_to_all.16 = f32[32,32,128]{2,1,0:T(8,128)S(1)} all-to-all(f32[32,32,128]{2,1,0:T(8,128)S(1)} %bitcast.23), channel_id=1, replica_groups=mesh['tm'=32,'space'=8] {'tm'}, dimensions={0} | all-to-all | bytes 1048576 | tf_op jit(solution)/shard_map/all_to_all | solution.py:508
  92.4 1.0 %shard_map.119 = (f32[2,4,8,1024]{3,2,1,0:T(8,128)}, f32[2,4,8,1024]{3,2,1,0:T(8,128)}) custom-call(f32[1024,128]{1,0:T(8,128)S(1)} %bitcast.22, f32[2,4,8,1024]{3,2,1,0:T(8,128)S(1)} %copy-done, f32[2,4,8,1024]{3,2,1,0:T(8,128)S(1)} %copy-done.1), custom_call_target="tpu_custom_call" | custom-call | flops 1000000 | bytes 2000000 | tf_op jit(solution)/shard_map/pallas_call | solution.py:373
  (27 shorter events, 0.1 us)
Async XLA Ops:
  2.0 8.0 %collective-permute-start = (f32[4,8,1024]{2,1,0:T(8,128)S(1)}, f32[4,8,1024]{2,1,0:T(8,128)S(1)}, u32[]{:S(2)}, u32[]{:S(2)}) collective-permute-start(f32[4,8,1024]{2,1,0:T(8,128)S(1)} %get-tuple-element.16), channel_id=1, source_target_pairs={{0,8},{8,16},{16,24},{24,32},{32,40},{40,48},{48,56},{56,64},{64,7... | collective-permute-start | bytes 393224 | tf_op jit(solution)/shard_map/ppermute | solution.py:394
  3.7 6.3 %collective-permute-start.1 = (f32[4,8,1024]{2,1,0:T(8,128)S(1)}, f32[4,8,1024]{2,1,0:T(8,128)S(1)}, u32[]{:S(2)}, u32[]{:S(2)}) collective-permute-start(f32[4,8,1024]{2,1,0:T(8,128)S(1)} %get-tuple-element.17), channel_id=1, source_target_pairs={{0,248},{8,0},{16,8},{24,16},{32,24},{40,32},{48,40},{56,48},{64,5... | collective-permute-start | bytes 393224 | tf_op jit(solution)/shard_map/ppermute | solution.py:394
  3.7 4.9 %collective-permute-start.2 = (f32[192,128]{1,0:T(8,128)S(1)}, f32[192,128]{1,0:T(8,128)S(1)}, u32[]{:S(2)}, u32[]{:S(2)}) collective-permute-start(f32[192,128]{1,0:T(8,128)S(1)} %get-tuple-element.14.to_down), channel_id=1, source_target_pairs={{0,1},{1,2},{2,3},{3,4},{4,5},{5,6},{6,7},{7,0},{8,9},{9,10},{10,1... | collective-permute-start | bytes 294920 | tf_op jit(solution)/shard_map/ppermute | solution.py:394
  5.9 4.0 %collective-permute-start.3 = (f32[192,128]{1,0:T(8,128)S(1)}, f32[192,128]{1,0:T(8,128)S(1)}, u32[]{:S(2)}, u32[]{:S(2)}) collective-permute-start(f32[192,128]{1,0:T(8,128)S(1)} %get-tuple-element.15.to_up), channel_id=1, source_target_pairs={{0,7},{1,0},{2,1},{3,2},{4,3},{5,4},{6,5},{7,6},{8,15},{9,8},{10,9... | collective-permute-start | bytes 294920 | tf_op jit(solution)/shard_map/ppermute | solution.py:394
  10.0 1.0 %copy-start.2 = (f32[128,1024]{1,0:T(8,128)S(1)}, f32[128,1024]{1,0:T(8,128)}, u32[]{:S(2)}) copy-start(f32[128,1024]{1,0:T(8,128)} %shard_map.113.partial) | copy-start | bytes 1572868
  12.2 35.7 %copy-start.5 = (bf16[512,512]{1,0:T(8,128)(2,1)S(1)}, bf16[512,512]{1,0:T(8,128)(2,1)}, u32[]{:S(2)}) copy-start(bf16[512,512]{1,0:T(8,128)(2,1)} %constant.29.clone.low_far) | copy-start | bytes 1572868
  12.2 35.7 %copy-start.6 = (bf16[512,512]{1,0:T(8,128)(2,1)S(1)}, bf16[512,512]{1,0:T(8,128)(2,1)}, u32[]{:S(2)}) copy-start(bf16[512,512]{1,0:T(8,128)(2,1)} %constant.28.clone.high_far) | copy-start | bytes 1572868
  12.2 35.7 %all-to-all-start = ((f32[32,48,128]{2,1,0:T(8,128)}), f32[32,48,128]{2,1,0:T(8,128)S(1)}, u32[]{:S(2)}, u32[]{:S(2)}) async-start(f32[32,48,128]{2,1,0:T(8,128)} %shard_map.115), calls=%async_computation | async-start | bytes 1572864 | tf_op jit(solution)/shard_map/all_to_all | solution.py:454
  47.9 3.8 %copy-start.8 = (f32[4,8,48]{1,0,2:T(4,128)S(1)}, f32[4,8,48]{1,0,2:T(4,128)}, u32[]{:S(2)}) copy-start(f32[4,8,48]{1,0,2:T(4,128)} %copy.17) | copy-start | bytes 18436
  47.9 3.8 %copy-start.9 = (f32[4,8,48]{1,0,2:T(4,128)S(1)}, f32[4,8,48]{1,0,2:T(4,128)}, u32[]{:S(2)}) copy-start(f32[4,8,48]{1,0,2:T(4,128)} %get-tuple-element.28) | copy-start | bytes 18436
  47.9 3.8 %copy-start.10 = (f32[4,8,48]{1,0,2:T(4,128)S(1)}, f32[4,8,48]{1,0,2:T(4,128)}, u32[]{:S(2)}) copy-start(f32[4,8,48]{1,0,2:T(4,128)} %get-tuple-element.29) | copy-start | bytes 18436
  50.5 1.7 %copy-start.7 = (f32[2,128]{1,0:T(2,128)S(1)}, f32[2,128]{1,0:T(2,128)}, u32[]{:S(2)}) copy-start(f32[2,128]{1,0:T(2,128)} %constant.30.clone.shifts) | copy-start | bytes 3076
  50.5 9.4 %collective-permute-start.4 = (f32[1344,128]{1,0:T(8,128)}, f32[1344,128]{1,0:T(8,128)S(1)}, u32[]{:S(2)}, u32[]{:S(2)}) collective-permute-start(f32[1344,128]{1,0:T(8,128)} %get-tuple-element.19), channel_id=1, source_target_pairs={{0,1},{1,2},{2,3},{3,4},{4,5},{5,6},{6,7},{7,0},{8,9},{9,10},{10,1... | collective-permute-start | bytes 2064392 | tf_op jit(solution)/shard_map/ppermute | solution.py:394
  51.7 10.4 %collective-permute-start.5 = (f32[1344,128]{1,0:T(8,128)S(1)}, f32[1344,128]{1,0:T(8,128)S(1)}, u32[]{:S(2)}, u32[]{:S(2)}) collective-permute-start(f32[1344,128]{1,0:T(8,128)S(1)} %get-tuple-element.20), channel_id=1, source_target_pairs={{0,7},{1,0},{2,1},{3,2},{4,3},{5,4},{6,5},{7,6},{8,15},{9,8},{10,9... | collective-permute-start | bytes 2064392 | tf_op jit(solution)/shard_map/ppermute | solution.py:394
  52.2 9.9 %copy-start.3 = (bf16[512,512]{1,0:T(8,128)(2,1)S(1)}, bf16[512,512]{1,0:T(8,128)(2,1)}, u32[]{:S(2)}) copy-start(bf16[512,512]{1,0:T(8,128)(2,1)} %constant.32.clone.low) | copy-start | bytes 1572868
  52.2 9.9 %copy-start.4 = (bf16[512,512]{1,0:T(8,128)(2,1)S(1)}, bf16[512,512]{1,0:T(8,128)(2,1)}, u32[]{:S(2)}) copy-start(bf16[512,512]{1,0:T(8,128)(2,1)} %constant.31.clone.high) | copy-start | bytes 1572868
  69.6 22.8 %copy-start = (f32[2,4,8,1024]{3,2,1,0:T(8,128)S(1)}, f32[2,4,8,1024]{3,2,1,0:T(8,128)}, u32[]{:S(2)}) copy-start(f32[2,4,8,1024]{3,2,1,0:T(8,128)} %state.1) | copy-start | bytes 786436
  69.6 22.8 %copy-start.1 = (f32[2,4,8,1024]{3,2,1,0:T(8,128)S(1)}, f32[2,4,8,1024]{3,2,1,0:T(8,128)}, u32[]{:S(2)}) copy-start(f32[2,4,8,1024]{3,2,1,0:T(8,128)} %adjoint.1) | copy-start | bytes 786436

commit v5 on v4

--- a/solution.py
+++ b/solution.py
@@ -284,7 +284,8 @@
     sub = lax.broadcasted_iota(jnp.int32, (SUBLANES, LANES), 0)
 
     def at(r, n):
-        return pl.ds(pl.multiple_of((r * 2 * count + n) * SUBLANES, SUBLANES), SUBLANES)
+        begin = (r * 2 * count + n) * SUBLANES
+        return pl.ds(begin if isinstance(r, int) else pl.multiple_of(begin, SUBLANES), SUBLANES)
 
     def solve(target, totals, r, m):
         a, b = scale[r, m], cross[r, m]
@@ -303,38 +304,42 @@
         lax.fori_loop(0, source.shape[0], start, None)
 
     def relax(old, new, r):
-        here = [[old[at(r, 2 * m + k), :] for k in range(2)] for m in range(count)]
+        def here(m):
+            return [old[at(r, 2 * m + k), :] for k in range(2)]
+
         for p in range(planes):
             base = p * strip
-            before = [pltpu.roll(v, 1, axis=0) for v in here[base + strip - 1]]
-            across = [pltpu.roll(v, LANES // 2, axis=1) for v in here[base + strip - 1]]
-            after = [pltpu.roll(v, SUBLANES - 1, axis=0) for v in here[base]]
+            before = [pltpu.roll(v, 1, axis=0) for v in here(base + strip - 1)]
+            across = [pltpu.roll(v, LANES // 2, axis=1) for v in here(base + strip - 1)]
+            after = [pltpu.roll(v, SUBLANES - 1, axis=0) for v in here(base)]
             after = [jnp.where(sub == SUBLANES - 1, x, v) for x, v in zip(across, after)]
             for c in range(strip):
                 m = base + c
                 flank = p * (strip + 1) + c
                 totals = []
                 for k in range(2):
-                    to_left = here[m - 1][k] if c else before[k]
-                    to_right = here[m + 1][k] if c < strip - 1 else after[k]
+                    to_left = here(m - 1)[k] if c else before[k]
+                    to_right = here(m + 1)[k] if c < strip - 1 else after[k]
                     total = w_col[r, flank] * to_left + w_col[r, flank + 1] * to_right
                     others = w_row[r, m] * old[at(r + 1, 2 * m + k), :] + w_row[r - 1, m] * old[at(r - 1, 2 * m + k), :]
                     mine = rhs[r, 2 * m + k]
                     if p:
-                        mine = mine + w_plane[r, m - strip] * here[m - strip][k]
+                        mine = mine + w_plane[r, m - strip] * here(m - strip)[k]
                     if p < planes - 1:
-                        others = others + w_plane[r, m] * here[m + strip][k]
+                        others = others + w_plane[r, m] * here(m + strip)[k]
                     totals.append(mine + (total + others))
                 solve(new, totals, r, m)
 
     old, new = first, second
     for sweep in range(1, SWEEPS):
-
-        def step(q, _, old=old, new=new, sweep=sweep):
-            relax(old, new, sweep + 2 * q)
-            relax(old, new, sweep + 2 * q + 1)
-
-        lax.fori_loop(0, (tall - 2 * sweep) // 2, step, None)
+        depth = tall - 2 * sweep
+        rows_a_turn = next(n for n in (5, 6, 4, 7, 2) if depth % n == 0)
+
+        def step(q, _, old=old, new=new, sweep=sweep, rows_a_turn=rows_a_turn):
+            for i in range(rows_a_turn):
+                relax(old, new, sweep + rows_a_turn * q + i)
+
+        lax.fori_loop(0, depth // rows_a_turn, step, None)
         old, new = new, old
 
     cells = planes * rows

time: 94 us -> 93.6 us (level)
  no operation moved by 1% of the time
where the time goes in v5:
time: 93.6 us; the launch traced here: 93 us
  waiting for transfers between devices  28.7 us (31%)
  blocking collectives  22.8 us (24%)
  Pallas kernels  20.3 us (22%)
  starting transfers between devices  17.2 us (18%)
  local copies, waits for them, and re-layouts  2.17 us (2%)
  other arithmetic  0.95 us (1%)
    all_to_all x1, blocking collectives, body(): got_back = lax.all_to_all(back, 'tm', 0, 0, tiled=True)  22.8 us
    all_to_all x1, waiting for transfers between devices, body(): lax.all_to_all(sent, 'tm', 0, 0, tiled=True).reshape(blocks * span, LANES)  22 us
    pallas_call x7, Pallas kernels, call(): pl.pallas_call(kernel, out_shape=outs, in_specs=[pl.BlockSpec(memory_spac...  20.3 us
    all_to_all x1, starting transfers between devices, body(): lax.all_to_all(sent, 'tm', 0, 0, tiled=True).reshape(blocks * span, LANES)  12 us
    ppermute x6, waiting for transfers between devices, shift(): lax.ppermute(block, axis, [(i, (i + distance) % count) for i in range(cou...  6.74 us
    ppermute x6, starting transfers between devices, shift(): lax.ppermute(block, axis, [(i, (i + distance) % count) for i in range(cou...  5.21 us
    unnamed x25, local copies, waits for them, and re-layouts  2.01 us
  transfers between devices with their start and end apart: 7, of which 4 were waited for; matrix products, arithmetic and copies ran while one was open for 2% of the time, Pallas kernels for 8%

profile of v5, /device:TPU:41, one launch (start us, length us, event | category | flops | bytes accessed | tf_op | source)
XLA Modules:
  0.0 93.0 jit_solution(15661541599308148649)
XLA Ops:
  0.6 1.3 %shard_map.114 = (f32[192,128]{1,0:T(8,128)S(1)}, f32[192,128]{1,0:T(8,128)S(1)}, f32[4,8,1024]{2,1,0:T(8,128)S(1)}, f32[4,8,1024]{2,1,0:T(8,128)S(1)}) custom-call(s32[1]{0:T(128)} %bitcast.1.me, f32[2,4,8,1024]{3,2,1,0:T(8,128)} %state.1, f32[2,4,8,1024]{3,2,1,0:T(8,128)} %adjoint.1, f32[4,8,1024]{2,1,0:T(8,128)} %cond_far.1), custom_call_target="tpu_custom_call" | custom-call | flops 100000 | bytes 1000000 | tf_op jit(solution)/shard_map/pallas_call | solution.py:378
  2.0 1.7 %collective-permute-start = (f32[4,8,1024]{2,1,0:T(8,128)S(1)}, f32[4,8,1024]{2,1,0:T(8,128)S(1)}, u32[]{:S(2)}, u32[]{:S(2)}) collective-permute-start(f32[4,8,1024]{2,1,0:T(8,128)S(1)} %get-tuple-element.16), channel_id=1, source_target_pairs={{0,8},{8,16},{16,24},{24,32},{32,40},{40,48},{48,56},{56,64},{64,7... | collective-permute-start | bytes 393224 | tf_op jit(solution)/shard_map/ppermute | solution.py:399
  3.7 0.0 collective-permute-start.1
  3.7 2.2 %collective-permute-start.2 = (f32[192,128]{1,0:T(8,128)S(1)}, f32[192,128]{1,0:T(8,128)S(1)}, u32[]{:S(2)}, u32[]{:S(2)}) collective-permute-start(f32[192,128]{1,0:T(8,128)S(1)} %get-tuple-element.14.to_down), channel_id=1, source_target_pairs={{0,1},{1,2},{2,3},{3,4},{4,5},{5,6},{6,7},{7,0},{8,9},{9,10},{10,1... | collective-permute-start | bytes 294920 | tf_op jit(solution)/shard_map/ppermute | solution.py:399
  5.9 2.7 %shard_map.113.partial = f32[128,1024]{1,0:T(8,128)} custom-call(f32[2,4,8,1024]{3,2,1,0:T(8,128)} %state.1, f32[2,4,8,1024]{3,2,1,0:T(8,128)} %adjoint.1, f32[2,4,8,1024]{3,2,1,0:T(8,128)} %refs_2_.1, f32[2,4,8,1024]{3,2,1,0:T(8,128)} %refs_3_.1, f32[4,8,1024]{2,1,0:T(8,128)} %cond_far.1), custom_call_target="tpu_custom_call" | custom-call | flops 10000000 | bytes 3000000 | tf_op jit(solution)/shard_map/pallas_call | solution.py:378
  8.6 0.0 collective-permute-done.2.top
  8.6 1.4 %collective-permute-done.3.bottom = f32[192,128]{1,0:T(8,128)S(1)} collective-permute-done((f32[192,128]{1,0:T(8,128)S(1)}, f32[192,128]{1,0:T(8,128)S(1)}, u32[]{:S(2)}, u32[]{:S(2)}) %collective-permute-start.3) | collective-permute-done | bytes 98336 | tf_op jit(solution)/shard_map/ppermute | solution.py:399
  10.0 0.0 collective-permute-done.prior
  10.0 1.0 %copy-done.2 = f32[128,1024]{1,0:T(8,128)S(1)} copy-done((f32[128,1024]{1,0:T(8,128)S(1)}, f32[128,1024]{1,0:T(8,128)}, u32[]{:S(2)}) %copy-start.2) | copy-done | bytes 524312
  11.0 1.2 %shard_map.115 = f32[32,48,128]{2,1,0:T(8,128)} custom-call(s32[1]{0:T(128)} %bitcast.place, f32[128,1024]{1,0:T(8,128)S(1)} %copy-done.2, f32[192,128]{1,0:T(8,128)S(1)} %get-tuple-element.14.to_down, f32[192,128]{1,0:T(8,128)S(1)} %get-tuple-element.15.to_up, f32[4,8,1024]{2,1,0:T(8,128)S(1)} %collective-permute-done.prior, ...), custom_call_target="tpu_custom_call" | custom-call | flops 10000000 | bytes 3000000 | tf_op jit(solution)/shard_map/pallas_call | solution.py:378
  12.2 12.0 %all-to-all-start = ((f32[32,48,128]{2,1,0:T(8,128)}), f32[32,48,128]{2,1,0:T(8,128)S(1)}, u32[]{:S(2)}, u32[]{:S(2)}) async-start(f32[32,48,128]{2,1,0:T(8,128)} %shard_map.115), calls=%async_computation | async-start | bytes 1572864 | tf_op jit(solution)/shard_map/all_to_all | solution.py:459
  24.2 0.1 copy.18
  24.3 0.7 copy.17
  25.1 0.1 copy.19
  25.2 0.7 broadcast_select_fusion
  25.9 22.0 %all-to-all-done = f32[32,48,128]{2,1,0:T(8,128)S(1)} async-done(((f32[32,48,128]{2,1,0:T(8,128)}), f32[32,48,128]{2,1,0:T(8,128)S(1)}, u32[]{:S(2)}, u32[]{:S(2)}) %all-to-all-start) | async-done | bytes 786464 | tf_op jit(solution)/shard_map/all_to_all | solution.py:459
  47.9 0.0 copy-start.10
  47.9 2.5 %shard_map.116 = (f32[1536,128]{1,0:T(8,128)S(1)}, f32[1344,128]{1,0:T(8,128)S(1)}, f32[1344,128]{1,0:T(8,128)}) custom-call(f32[1536,128]{1,0:T(8,128)S(1)} %bitcast.24, bf16[512,512]{1,0:T(8,128)(2,1)S(1)} %copy-done.6, bf16[512,512]{1,0:T(8,128)(2,1)S(1)} %copy-done.5), custom_call_target="tpu_custom_call" | custom-call | flops 600000000 | bytes 4000000 | tf_op jit(solution)/shard_map/pallas_call | solution.py:378
  50.5 0.0 copy-start.7
  50.5 1.2 %collective-permute-start.4 = (f32[1344,128]{1,0:T(8,128)}, f32[1344,128]{1,0:T(8,128)S(1)}, u32[]{:S(2)}, u32[]{:S(2)}) collective-permute-start(f32[1344,128]{1,0:T(8,128)} %get-tuple-element.19), channel_id=1, source_target_pairs={{0,1},{1,2},{2,3},{3,4},{4,5},{5,6},{6,7},{7,0},{8,9},{9,10},{10,1... | collective-permute-start | bytes 2064392 | tf_op jit(solution)/shard_map/ppermute | solution.py:399
  51.8 0.2 pad_maximum_fusion
  52.0 0.1 copy.16
  52.2 0.0 copy-start.3
  52.2 0.0 copy-start.4
  52.2 4.5 %shard_map.117 = (f32[22,12,8,128]{3,2,1,0:T(8,128)S(1)}, f32[22,16,8,128]{3,2,1,0:T(8,128)S(1)}, f32[22,9,8,128]{3,2,1,0:T(8,128)S(1)}, f32[22,12,8,128]{3,2,1,0:T(8,128)S(1)}, f32[22,12,8,128]{3,2,1,0:T(8,128)S(1)}) custom-call(f32[24,8,128]{2,1,0:T(8,128)S(1)} %pad.4.kappa, f32[2,128]{1,0:T(2,128)S(1)} %copy-done.7), custom_call_target="tpu_custom_call" | custom-call | flops 1000000000 | bytes 10000000 | tf_op jit(solution)/shard_map/pallas_call | solution.py:378
  56.7 3.2 %collective-permute-done.4 = f32[1344,128]{1,0:T(8,128)S(1)} collective-permute-done((f32[1344,128]{1,0:T(8,128)}, f32[1344,128]{1,0:T(8,128)S(1)}, u32[]{:S(2)}, u32[]{:S(2)}) %collective-permute-start.4) | collective-permute-done | bytes 688160 | tf_op jit(solution)/shard_map/ppermute | solution.py:399
  59.9 2.2 %collective-permute-done.5 = f32[1344,128]{1,0:T(8,128)S(1)} collective-permute-done((f32[1344,128]{1,0:T(8,128)S(1)}, f32[1344,128]{1,0:T(8,128)S(1)}, u32[]{:S(2)}, u32[]{:S(2)}) %collective-permute-start.5) | collective-permute-done | bytes 688160 | tf_op jit(solution)/shard_map/ppermute | solution.py:399
  62.1 7.1 %shard_map.118 = f32[1024,128]{1,0:T(8,128)S(1)} custom-call(f32[8,24,8,128]{3,2,1,0:T(8,128)S(1)} %bitcast.25, f32[7,24,8,128]{3,2,1,0:T(8,128)S(1)} %bitcast.26, f32[7,24,8,128]{3,2,1,0:T(8,128)S(1)} %bitcast.27, f32[22,12,8,128]{3,2,1,0:T(8,128)S(1)} %get-tuple-element.21.w_row, f32[22,16,8,128]{3,2,1,0:T(8,128)S(1)} %get-tuple-element.22.w_col, ...), custom_call_target="tpu_custom_call" | custom-call | flops 1000000000 | bytes 6000000 | tf_op jit(solution)/shard_map/pallas_call | solution.py:378
  69.2 0.0 copy-start
  69.2 0.0 copy-start.1
  69.2 22.8 %all_to_all.16 = f32[32,32,128]{2,1,0:T(8,128)S(1)} all-to-all(f32[32,32,128]{2,1,0:T(8,128)S(1)} %bitcast.23), channel_id=1, replica_groups=mesh['tm'=32,'space'=8] {'tm'}, dimensions={0} | all-to-all | bytes 1048576 | tf_op jit(solution)/shard_map/all_to_all | solution.py:513
  92.0 1.0 %shard_map.119 = (f32[2,4,8,1024]{3,2,1,0:T(8,128)}, f32[2,4,8,1024]{3,2,1,0:T(8,128)}) custom-call(f32[1024,128]{1,0:T(8,128)S(1)} %bitcast.22, f32[2,4,8,1024]{3,2,1,0:T(8,128)S(1)} %copy-done, f32[2,4,8,1024]{3,2,1,0:T(8,128)S(1)} %copy-done.1), custom_call_target="tpu_custom_call" | custom-call | flops 1000000 | bytes 2000000 | tf_op jit(solution)/shard_map/pallas_call | solution.py:378
  (27 shorter events, 0.1 us)
Async XLA Ops:
  2.0 8.0 %collective-permute-start = (f32[4,8,1024]{2,1,0:T(8,128)S(1)}, f32[4,8,1024]{2,1,0:T(8,128)S(1)}, u32[]{:S(2)}, u32[]{:S(2)}) collective-permute-start(f32[4,8,1024]{2,1,0:T(8,128)S(1)} %get-tuple-element.16), channel_id=1, source_target_pairs={{0,8},{8,16},{16,24},{24,32},{32,40},{40,48},{48,56},{56,64},{64,7... | collective-permute-start | bytes 393224 | tf_op jit(solution)/shard_map/ppermute | solution.py:399
  3.7 6.3 %collective-permute-start.1 = (f32[4,8,1024]{2,1,0:T(8,128)S(1)}, f32[4,8,1024]{2,1,0:T(8,128)S(1)}, u32[]{:S(2)}, u32[]{:S(2)}) collective-permute-start(f32[4,8,1024]{2,1,0:T(8,128)S(1)} %get-tuple-element.17), channel_id=1, source_target_pairs={{0,248},{8,0},{16,8},{24,16},{32,24},{40,32},{48,40},{56,48},{64,5... | collective-permute-start | bytes 393224 | tf_op jit(solution)/shard_map/ppermute | solution.py:399
  3.7 4.9 %collective-permute-start.2 = (f32[192,128]{1,0:T(8,128)S(1)}, f32[192,128]{1,0:T(8,128)S(1)}, u32[]{:S(2)}, u32[]{:S(2)}) collective-permute-start(f32[192,128]{1,0:T(8,128)S(1)} %get-tuple-element.14.to_down), channel_id=1, source_target_pairs={{0,1},{1,2},{2,3},{3,4},{4,5},{5,6},{6,7},{7,0},{8,9},{9,10},{10,1... | collective-permute-start | bytes 294920 | tf_op jit(solution)/shard_map/ppermute | solution.py:399
  5.9 4.0 %collective-permute-start.3 = (f32[192,128]{1,0:T(8,128)S(1)}, f32[192,128]{1,0:T(8,128)S(1)}, u32[]{:S(2)}, u32[]{:S(2)}) collective-permute-start(f32[192,128]{1,0:T(8,128)S(1)} %get-tuple-element.15.to_up), channel_id=1, source_target_pairs={{0,7},{1,0},{2,1},{3,2},{4,3},{5,4},{6,5},{7,6},{8,15},{9,8},{10,9... | collective-permute-start | bytes 294920 | tf_op jit(solution)/shard_map/ppermute | solution.py:399
  10.0 1.0 %copy-start.2 = (f32[128,1024]{1,0:T(8,128)S(1)}, f32[128,1024]{1,0:T(8,128)}, u32[]{:S(2)}) copy-start(f32[128,1024]{1,0:T(8,128)} %shard_map.113.partial) | copy-start | bytes 1572868
  12.2 35.7 %copy-start.5 = (bf16[512,512]{1,0:T(8,128)(2,1)S(1)}, bf16[512,512]{1,0:T(8,128)(2,1)}, u32[]{:S(2)}) copy-start(bf16[512,512]{1,0:T(8,128)(2,1)} %constant.29.clone.low_far) | copy-start | bytes 1572868
  12.2 35.7 %copy-start.6 = (bf16[512,512]{1,0:T(8,128)(2,1)S(1)}, bf16[512,512]{1,0:T(8,128)(2,1)}, u32[]{:S(2)}) copy-start(bf16[512,512]{1,0:T(8,128)(2,1)} %constant.28.clone.high_far) | copy-start | bytes 1572868
  12.2 35.7 %all-to-all-start = ((f32[32,48,128]{2,1,0:T(8,128)}), f32[32,48,128]{2,1,0:T(8,128)S(1)}, u32[]{:S(2)}, u32[]{:S(2)}) async-start(f32[32,48,128]{2,1,0:T(8,128)} %shard_map.115), calls=%async_computation | async-start | bytes 1572864 | tf_op jit(solution)/shard_map/all_to_all | solution.py:459
  47.9 3.8 %copy-start.8 = (f32[4,8,48]{1,0,2:T(4,128)S(1)}, f32[4,8,48]{1,0,2:T(4,128)}, u32[]{:S(2)}) copy-start(f32[4,8,48]{1,0,2:T(4,128)} %copy.17) | copy-start | bytes 18436
  47.9 3.8 %copy-start.9 = (f32[4,8,48]{1,0,2:T(4,128)S(1)}, f32[4,8,48]{1,0,2:T(4,128)}, u32[]{:S(2)}) copy-start(f32[4,8,48]{1,0,2:T(4,128)} %get-tuple-element.28) | copy-start | bytes 18436
  47.9 3.8 %copy-start.10 = (f32[4,8,48]{1,0,2:T(4,128)S(1)}, f32[4,8,48]{1,0,2:T(4,128)}, u32[]{:S(2)}) copy-start(f32[4,8,48]{1,0,2:T(4,128)} %get-tuple-element.29) | copy-start | bytes 18436
  50.5 1.7 %copy-start.7 = (f32[2,128]{1,0:T(2,128)S(1)}, f32[2,128]{1,0:T(2,128)}, u32[]{:S(2)}) copy-start(f32[2,128]{1,0:T(2,128)} %constant.30.clone.shifts) | copy-start | bytes 3076
  50.5 9.4 %collective-permute-start.4 = (f32[1344,128]{1,0:T(8,128)}, f32[1344,128]{1,0:T(8,128)S(1)}, u32[]{:S(2)}, u32[]{:S(2)}) collective-permute-start(f32[1344,128]{1,0:T(8,128)} %get-tuple-element.19), channel_id=1, source_target_pairs={{0,1},{1,2},{2,3},{3,4},{4,5},{5,6},{6,7},{7,0},{8,9},{9,10},{10,1... | collective-permute-start | bytes 2064392 | tf_op jit(solution)/shard_map/ppermute | solution.py:399
  51.7 10.4 %collective-permute-start.5 = (f32[1344,128]{1,0:T(8,128)S(1)}, f32[1344,128]{1,0:T(8,128)S(1)}, u32[]{:S(2)}, u32[]{:S(2)}) collective-permute-start(f32[1344,128]{1,0:T(8,128)S(1)} %get-tuple-element.20), channel_id=1, source_target_pairs={{0,7},{1,0},{2,1},{3,2},{4,3},{5,4},{6,5},{7,6},{8,15},{9,8},{10,9... | collective-permute-start | bytes 2064392 | tf_op jit(solution)/shard_map/ppermute | solution.py:399
  52.2 9.9 %copy-start.3 = (bf16[512,512]{1,0:T(8,128)(2,1)S(1)}, bf16[512,512]{1,0:T(8,128)(2,1)}, u32[]{:S(2)}) copy-start(bf16[512,512]{1,0:T(8,128)(2,1)} %constant.32.clone.low) | copy-start | bytes 1572868
  52.2 9.9 %copy-start.4 = (bf16[512,512]{1,0:T(8,128)(2,1)S(1)}, bf16[512,512]{1,0:T(8,128)(2,1)}, u32[]{:S(2)}) copy-start(bf16[512,512]{1,0:T(8,128)(2,1)} %constant.31.clone.high) | copy-start | bytes 1572868
  69.2 22.8 %copy-start = (f32[2,4,8,1024]{3,2,1,0:T(8,128)S(1)}, f32[2,4,8,1024]{3,2,1,0:T(8,128)}, u32[]{:S(2)}) copy-start(f32[2,4,8,1024]{3,2,1,0:T(8,128)} %state.1) | copy-start | bytes 786436
  69.2 22.8 %copy-start.1 = (f32[2,4,8,1024]{3,2,1,0:T(8,128)S(1)}, f32[2,4,8,1024]{3,2,1,0:T(8,128)}, u32[]{:S(2)}) copy-start(f32[2,4,8,1024]{3,2,1,0:T(8,128)} %adjoint.1) | copy-start | bytes 786436
